TPU v7x, 256 devices: a whole 4x4x8 slice. The times are simulated.
256 devices in a mesh: vol: 64 (over x_hi, z, y), tilt: 4 (over x_lo, core).
Axes of the slice: x: 4 (x_hi: 2, x_lo: 2; x = x_hi * 2 + x_lo), y: 4, z: 8, core: 2. Of those that a mesh axis runs over, the one named last changes fastest.
Arguments:
- images: bfloat16 [64, 128, 4096], P('tilt', 'vol'), may hold values from -6 to 6
- angle_tenths: int32 [64], P('tilt'), may hold values from -600 to 600
- dose_index: int32 [64], P('tilt'), may hold values from 0 to 120
- box_corner: int32 [3, 512], P(None, 'vol'), may hold values from 0 to 4032, as said below
- box_owner: int32 [512, 1], P('vol'), may hold values from 0 to 3; in each aligned block of 8 rows (0 to 7, 8 to 15, ...) at most 4 rows name the same one
Outputs:
- volume: bfloat16 [128, 4096, 128], P('tilt', 'vol')
- box_slots: bfloat16 [64, 4, 4, 64, 4096], P('vol', 'tilt')
Inputs may be any that keep to these rules, and one draw needn't show every extreme that they name: `box_corner`: column r holds the corner x, y, z of a box. Its x lies in x-block r // 8, from (r // 8) * 64 to (r // 8) * 64 + 63, and is at most 4032; its y is at most 64 and its z at most 64. `box_owner`: within the rows of one device no owner is named more than 4 times.
All inputs are finite; a program needn't handle non-finite values.
Results may differ from a plain program's by a relative error of at most 0.014.
Values may be sent and summed in bfloat16 or wider, within the bound.
A program may use at most 192 MiB of HBM per device.

v0:
```python
import functools
import math

import jax
import jax.numpy as jnp
import ml_dtypes
import numpy as np
from jax import lax
from jax.experimental import pallas as pl
from jax.experimental.pallas import tpu as pltpu
from jax.sharding import PartitionSpec as P

MESH = pl.DeviceIdType.MESH
BF = jnp.bfloat16
F32 = jnp.float32

PIX = 4096
EDGE = 64
COLS = 64
DEPTH = 128
BOX = 64
BLOCKS = 64
TILTS_HERE = 16
TILTS = 64
ROWS_MSG = 48
BAND = 192
TILE = 16
WIN = 32
CHUNK = 8
NCHUNK = TILTS // CHUNK
CELLS = 2 * COLS * DEPTH

VMEM_LIMIT = 56 * 1024 * 1024


def split_np(table):
    high = table.astype(np.float32).astype(ml_dtypes.bfloat16)
    low = (table - high.astype(np.float64)).astype(np.float32).astype(ml_dtypes.bfloat16)
    return high, low


def fft_tables():
    grid = np.outer(np.arange(EDGE), np.arange(EDGE))
    cos_t = np.cos(2 * np.pi * (grid % EDGE) / EDGE)
    sin_t = np.sin(2 * np.pi * (grid % EDGE) / EDGE)
    stacked = np.concatenate([cos_t, sin_t], axis=0)
    s_hi, s_lo = split_np(stacked)
    left = np.concatenate([s_hi, s_lo], axis=0)
    two = np.eye(2)
    cos2, sin2 = np.kron(two, cos_t), np.kron(two, sin_t)
    fwd = np.block([[cos2, -sin2], [sin2, cos2]])
    inv = np.block([[cos2, sin2], [-sin2, cos2]])
    f_hi, f_lo = split_np(fwd)
    i_hi, i_lo = split_np(inv)
    right = np.stack([f_hi, f_lo, i_hi, i_lo])
    twist = np.stack([np.cos(2 * np.pi * grid / PIX), np.sin(2 * np.pi * grid / PIX)])
    twist = np.concatenate([twist, twist], axis=2).astype(np.float32)
    k1, k2 = np.meshgrid(np.arange(EDGE), np.arange(EDGE), indexing="ij")
    freq = k1 + EDGE * k2
    freq = np.minimum(freq, PIX - freq)
    ratio = 2.0 * freq / PIX
    bend = ratio * np.sqrt(ratio)
    ramp = np.where(freq * 2 == PIX, 0.0, freq / PIX) / PIX
    shape = np.stack([bend, ramp])
    shape = np.concatenate([shape, shape], axis=2).astype(np.float32)
    return left, right, twist, shape


def dot(a, b):
    return jnp.dot(a, b, preferred_element_type=F32)


def dot_t(a, b):
    return lax.dot_general(a, b, (((1,), (1,)), ((), ())), preferred_element_type=F32)


def halves(value):
    high = value.astype(BF)
    return high, (value - high.astype(F32)).astype(BF)


def filter_kernel(
    x_ref, left_ref, right_ref, twist_ref, shape_ref, dose_ref, quot_ref, rest_ref, meta_ref, out_ref, scr
):
    left = left_ref[...]
    cos_w, sin_w = twist_ref[0], twist_ref[1]
    bend, ramp = shape_ref[0], shape_ref[1]
    lane = lax.broadcasted_iota(jnp.int32, (EDGE, 128), 1)
    first = lane < EDGE
    n1 = lax.broadcasted_iota(jnp.int32, (BLOCKS, EDGE), 1)
    for pair in range(TILTS_HERE // 2):
        part = dot(left, x_ref[pair])
        cx = part[0:64] + part[128:192]
        sx = part[64:128] + part[192:256]
        re = cx[:, :128] + sx[:, 128:]
        im = cx[:, 128:] - sx[:, :128]
        turned = jnp.concatenate([re * cos_w + im * sin_w, im * cos_w - re * sin_w], axis=1)
        hi, lo = halves(turned)
        spec = dot(hi, right_ref[0]) + (dot(lo, right_ref[0]) + dot(hi, right_ref[1]))
        resp = ramp * jnp.exp((-0.05 * dose_ref[pair : pair + 1, :]) * bend)
        spec = spec * jnp.concatenate([resp, resp], axis=1)
        hi, lo = halves(spec)
        back = dot(hi, right_ref[2]) + (dot(lo, right_ref[2]) + dot(hi, right_ref[3]))
        re, im = back[:, :128], back[:, 128:]
        turned = jnp.concatenate([re * cos_w - im * sin_w, im * cos_w + re * sin_w], axis=1)
        hi, lo = halves(turned)
        part = dot(left, hi)
        extra = dot(left[0:128], lo)
        cx = part[0:64] + (part[128:192] + extra[0:64])
        sx = part[64:128] + (part[192:256] + extra[64:128])
        re = cx[:, :128] - sx[:, 128:]
        im = cx[:, 128:] + sx[:, :128]
        rows = (
            jnp.where(first, re, pltpu.roll(im, EDGE, 1)),
            jnp.where(first, pltpu.roll(re, EDGE, 1), im),
        )
        for half in range(2):
            tilt = 2 * pair + half
            image = rows[half].astype(BF)
            quot = quot_ref[:, tilt : tilt + 1]
            rest = rest_ref[:, tilt : tilt + 1]
            pick = jnp.concatenate(
                [(n1 == quot + step).astype(F32).astype(BF) for step in range(4)], axis=0
            )
            near = dot(pick, image)
            at = (lane & EDGE) | ((lane + rest) & (EDGE - 1))
            stay = (lane & (EDGE - 1)) + rest < EDGE
            moved = [
                jnp.take_along_axis(near[step * EDGE : (step + 1) * EDGE], at, axis=1)
                for step in range(4)
            ]
            for step in range(3):
                piece = jnp.where(stay, moved[step], moved[step + 1])
                if step == 2:
                    for place in range(2):
                        piece = jnp.where(lane == 60 + place, meta_ref[place, tilt : tilt + 1, 0:1], piece)
                    piece = jnp.where(lane == 62, quot.astype(F32), piece)
                    piece = jnp.where(lane == 63, rest.astype(F32), piece)
                scr[pl.ds(tilt * 3 + step, BLOCKS, stride=ROWS_MSG), :] = piece
    for block in range(BLOCKS):
        out_ref[block] = scr[block * ROWS_MSG : (block + 1) * ROWS_MSG, :].astype(BF)


def exchange_kernel(x_ref, o_ref, loc_sem, a_send, a_recv, x_send, x_recv, m_send, m_recv):
    v = lax.axis_index("vol")
    t = lax.axis_index("tilt")
    y, z, xh = lax.rem(v, 4), lax.rem(v // 4, 8), v // 32
    core, xl = lax.rem(t, 2), t // 2
    mate = xl * 2 + (1 - core)
    cross = (1 - xl) * 2 + core
    barrier = pltpu.get_barrier_semaphore()

    def greet(i, carry):
        p = lax.rem(xh * 32 + i, 64)
        q = jnp.where(i < 32, t, cross)

        @pl.when(p != v)
        def _():
            pl.semaphore_signal(barrier, inc=1, device_id=(p, q), device_id_type=MESH)

        return carry

    lax.fori_loop(0, 64, greet, 0)
    pl.semaphore_signal(barrier, inc=1, device_id=(v, cross), device_id_type=MESH)
    pl.semaphore_signal(barrier, inc=1, device_id=(v, mate), device_id_type=MESH)
    pl.semaphore_wait(barrier, 65)

    own = pltpu.make_async_copy(x_ref.at[v], o_ref.at[t, v], loc_sem)
    own.start()
    steps = (0, 1, 7, 2, 6, 3, 5, 4)
    for dz in steps:
        for far in range(2):
            for dy in range(4):
                if dz == 0 and far == 0 and dy == 0:
                    continue
                zz, yy = lax.rem(z + dz, 8), lax.rem(y + dy, 4)
                p = (xh if far == 0 else 1 - xh) * 32 + zz * 4 + yy
                pltpu.make_async_remote_copy(
                    x_ref.at[p],
                    o_ref.at[t, v],
                    a_send,
                    a_recv.at[far, z],
                    device_id=(p, t if far == 0 else cross),
                    device_id_type=MESH,
                ).start()
    for dz in steps:
        for far in range(2):
            zz = lax.rem(z + 8 - dz, 8)
            base = (xh if far == 0 else 1 - xh) * 32 + zz * 4
            slot = t if far == 0 else cross
            number = 4
            if dz == 0 and far == 0:
                own.wait()
                number = 3
            pltpu.make_async_copy(
                o_ref.at[slot, pl.ds(base, number)], o_ref.at[slot, pl.ds(base, number)], a_recv.at[far, zz]
            ).wait()
            block = o_ref.at[slot, pl.ds(base, 4)]
            pltpu.make_async_remote_copy(
                block, block, x_send, x_recv.at[far, zz], device_id=(v, cross), device_id_type=MESH
            ).start()
            pltpu.make_async_remote_copy(
                block, block, m_send, m_recv.at[0, far, zz], device_id=(v, mate), device_id_type=MESH
            ).start()
    for dz in steps:
        for far in range(2):
            zz = lax.rem(z + 8 - dz, 8)
            base = (xh if far == 0 else 1 - xh) * 32 + zz * 4
            slot = cross if far == 0 else t
            block = o_ref.at[slot, pl.ds(base, 4)]
            pltpu.make_async_copy(block, block, x_recv.at[far, zz]).wait()
            pltpu.make_async_remote_copy(
                block, block, m_send, m_recv.at[1, far, zz], device_id=(v, mate), device_id_type=MESH
            ).start()
    mate_cross = (1 - xl) * 2 + (1 - core)
    for kind in range(2):
        for far in range(2):
            for zz in range(8):
                base = (xh if far == 0 else 1 - xh) * 32 + zz * 4
                slot = mate if (kind + far) % 2 == 0 else mate_cross
                block = o_ref.at[slot, pl.ds(base, 4)]
                pltpu.make_async_copy(block, block, m_recv.at[kind, far, zz]).wait()
    pltpu.make_async_copy(x_ref.at[pl.ds(0, 63)], x_ref.at[pl.ds(0, 63)], a_send).wait()
    half = o_ref.at[0]
    pltpu.make_async_copy(half, half, x_send).wait()
    both = o_ref.at[pl.ds(0, 2)]
    pltpu.make_async_copy(both, both, m_send).wait()


def project_kernel(recv_ref, start_ref, cst_ref, trig_ref, part, scr, win):
    lane = lax.broadcasted_iota(jnp.int32, (BLOCKS, 128), 1)
    low = lane < EDGE
    fold = (
        lax.broadcasted_iota(jnp.int32, (EDGE, 128), 0) == (lane & (EDGE - 1))
    ).astype(F32).astype(BF)

    for group in range(4):
        scr[group * 3072 : (group + 1) * 3072, :] = recv_ref[group].reshape(3072, 128).astype(F32)

    def turn(tilt, carry):
        group, inner = tilt // TILTS_HERE, lax.rem(tilt, TILTS_HERE)
        parts = []
        for step in range(3):
            piece = scr[pl.ds(group * 3072 + inner * 3 + step, BLOCKS, stride=ROWS_MSG), :]
            wide = jnp.concatenate([jnp.where(low, piece, 0.0), jnp.where(low, 0.0, piece)], axis=0)
            parts.append(dot_t(fold, wide.astype(BF)))
        whole = jnp.concatenate(parts, axis=0)
        moved = jnp.concatenate([whole[8:], jnp.zeros((8, 128), F32)], axis=0)
        at = pl.multiple_of(tilt * 2 * BAND, BAND)
        win[pl.ds(at, BAND), :] = whole.astype(BF)
        win[pl.ds(at + BAND, BAND), :] = moved.astype(BF)
        return carry

    lax.fori_loop(0, TILTS, turn, 0, unroll=4)

    zcol = lax.broadcasted_iota(jnp.int32, (TILE, CHUNK * WIN), 0).astype(F32)

    def tile(xt, zt, carry):
        number = xt * 8 + zt
        total = jnp.zeros((TILE * TILE, 128), F32)
        for chunk in range(NCHUNK):
            right = jnp.concatenate(
                [
                    win[pl.ds(pl.multiple_of(start_ref[number, chunk * CHUNK + i], 16), WIN), :]
                    for i in range(CHUNK)
                ],
                axis=0,
            )
            cos_l = trig_ref[chunk : chunk + 1, :]
            sin_l = trig_ref[NCHUNK + chunk : NCHUNK + chunk + 1, :]
            here = zcol * sin_l + cst_ref[pl.ds(number * NCHUNK + chunk, 1), :]
            pieces = []
            for _ in range(TILE):
                pieces.append(jnp.maximum(1.0 - jnp.abs(here), 0.0).astype(BF))
                here = here + cos_l
            total = total + dot(jnp.concatenate(pieces, axis=0), right)
        rounded = total.astype(BF)
        for i in range(TILE):
            at = pl.multiple_of((xt * TILE + i) * DEPTH + zt * TILE, TILE)
            part[pl.ds(at, TILE), :] = rounded[i * TILE : (i + 1) * TILE]
        return carry

    for xt in range(4):
        lax.fori_loop(0, 8, functools.partial(tile, xt), 0)


def mate_kernel(x_ref, o_ref, send, recv):
    v = lax.axis_index("vol")
    t = lax.axis_index("tilt")
    mate = (t // 2) * 2 + (1 - lax.rem(t, 2))
    barrier = pltpu.get_barrier_semaphore()
    pl.semaphore_signal(barrier, inc=1, device_id=(v, mate), device_id_type=MESH)
    pl.semaphore_wait(barrier, 1)
    there = pltpu.make_async_remote_copy(
        x_ref, o_ref, send, recv, device_id=(v, mate), device_id_type=MESH
    )
    there.start()
    there.wait()


def box_kernel(own_ref, other_ref, slot_ref, box_ref, vol_ref, ext_ref, sem):
    core = slot_ref[17]
    half = CELLS // 2
    here = pltpu.make_async_copy(
        own_ref, ext_ref.at[pl.ds(pl.multiple_of(core * half, half), half)], sem.at[0]
    )
    there = pltpu.make_async_copy(
        other_ref, ext_ref.at[pl.ds(pl.multiple_of((1 - core) * half, half), half)], sem.at[1]
    )
    here.start()
    there.start()
    here.wait()
    there.wait()
    lane = lax.broadcasted_iota(jnp.int32, (BOX, 128), 1)
    low = lane < BOX
    y_of = (lane & 63) * 2 + (lane >> 6)
    line = lax.broadcasted_iota(jnp.int32, (BOX, 128), 0)
    quarter = (y_of == line + slot_ref[16]).astype(F32).astype(BF)[0:32]

    def slab(i, carry):
        rows = ext_ref[pl.ds(pl.multiple_of(i * 256, 256), 256), :]
        vol_ref[:, pl.ds(pl.multiple_of(i * 256, 256), 256)] = dot_t(quarter, rows).astype(BF)
        return carry

    lax.fori_loop(0, COLS // 2, slab, 0, unroll=4)

    for slot in range(4):
        x0, y0, z0 = slot_ref[slot * 4 + 1], slot_ref[slot * 4 + 2], slot_ref[slot * 4 + 3]
        present = slot_ref[slot * 4]
        chosen = ((y_of == line + y0) & (present > 0)).astype(F32).astype(BF)
        even_by = lax.rem(128 - z0, 128)
        odd_by = lax.rem(192 - z0, 128)

        def cut(i, carry):
            rows = ext_ref[pl.ds(pl.multiple_of((x0 + 2 * i) * DEPTH, DEPTH), 2 * DEPTH), :]
            both = dot_t(chosen, rows)
            even = pltpu.roll(both[:, :128], even_by, 1)
            odd = pltpu.roll(both[:, 128:], odd_by, 1)
            box_ref[slot, :, pl.ds(pl.multiple_of(i * 128, 128), 128)] = jnp.where(
                low, even, odd
            ).astype(BF)
            return carry

        lax.fori_loop(0, BOX // 2, cut, 0, unroll=4)


def trig_of(tenths):
    angle = tenths.astype(F32) * (math.pi / 1800.0)
    return jnp.cos(angle), jnp.sin(angle)


def per_device(images, angle_tenths, dose_index, box_corner, box_owner):
    x_block = lax.axis_index("vol")
    group = lax.axis_index("tilt")
    core = lax.rem(group, 2)
    vm = pl.BlockSpec(memory_space=pltpu.VMEM)
    sm = pl.BlockSpec(memory_space=pltpu.SMEM)
    anym = pl.BlockSpec(memory_space=pl.ANY)

    cosine, sine = trig_of(angle_tenths)
    columns = jnp.arange(BLOCKS, dtype=jnp.int32).astype(F32)[:, None] * COLS
    lowest = (
        PIX / 2
        + (columns - PIX / 2) * cosine[None, :]
        + jnp.minimum(-(DEPTH / 2) * sine, (DEPTH / 2 - 1) * sine)[None, :]
    )
    begin = jnp.floor(lowest).astype(jnp.int32) - 1
    quot, rest = begin >> 6, begin & 63
    meta = jnp.stack([angle_tenths >> 5, angle_tenths & 31]).astype(F32)
    meta = jnp.broadcast_to(meta[:, :, None], (2, TILTS_HERE, 128))
    dose = jnp.repeat(dose_index.astype(F32).reshape(TILTS_HERE // 2, 2), EDGE, axis=1)
    cube = images.reshape(TILTS_HERE // 2, 2, 2, EDGE, EDGE).transpose(0, 3, 2, 1, 4)
    cube = cube.reshape(TILTS_HERE // 2, EDGE, 4 * EDGE)
    tables = [jnp.asarray(a) for a in fft_tables()]
    outgoing = pl.pallas_call(
        filter_kernel,
        out_shape=jax.ShapeDtypeStruct((BLOCKS, ROWS_MSG, 128), BF),
        in_specs=[vm] * 9,
        out_specs=vm,
        scratch_shapes=[pltpu.VMEM((BLOCKS * ROWS_MSG, 128), F32)],
        compiler_params=pltpu.CompilerParams(vmem_limit_bytes=VMEM_LIMIT),
        name="filter",
    )(cube, *tables, dose, quot, rest, meta)

    dma = pltpu.SemaphoreType.DMA
    recv = pl.pallas_call(
        exchange_kernel,
        out_shape=jax.ShapeDtypeStruct((4, BLOCKS, ROWS_MSG, 128), BF),
        in_specs=[anym],
        out_specs=anym,
        scratch_shapes=[dma, dma, dma((2, 8)), dma, dma((2, 8)), dma, dma((2, 2, 8))],
        compiler_params=pltpu.CompilerParams(collective_id=1, has_side_effects=True),
        name="exchange",
    )(outgoing)

    heads = recv[:, 0].reshape(TILTS, 3, 128)[:, 2, 60:64].astype(jnp.int32)
    tenths = heads[:, 0] * 32 + heads[:, 1]
    base = heads[:, 2] * 64 + heads[:, 3]
    cos_all, sin_all = trig_of(tenths)
    number = jnp.arange(32, dtype=jnp.int32)
    x_tile = (x_block * COLS + core * COLS + (number // 8) * TILE).astype(F32)
    z_tile = ((number % 8) * TILE).astype(F32)
    coord = (
        PIX / 2
        + (x_tile[:, None] - PIX / 2) * cos_all[None, :]
        + (z_tile[:, None] - DEPTH / 2) * sin_all[None, :]
    )
    least = coord + jnp.minimum((TILE - 1) * sin_all, 0.0)[None, :]
    local = jnp.clip(jnp.floor(least).astype(jnp.int32) - base[None, :], 0, BAND - WIN)
    local8 = local & -8
    odd = (local8 >> 3) & 1
    tilt_number = jnp.arange(TILTS, dtype=jnp.int32)[None, :]
    start = (tilt_number * 2 + odd) * BAND + local8 - 8 * odd
    offset = coord - (base[None, :] + local8).astype(F32)
    pixel = jnp.arange(WIN, dtype=jnp.int32).astype(F32)
    cst = (offset[:, :, None] - pixel).reshape(32 * NCHUNK, CHUNK * WIN)
    trig = jnp.stack([cos_all, sin_all])
    trig = jnp.repeat(trig.reshape(2 * NCHUNK, CHUNK), WIN, axis=1)
    part = pl.pallas_call(
        project_kernel,
        out_shape=jax.ShapeDtypeStruct((CELLS // 2, 128), BF),
        in_specs=[vm, sm, vm, vm],
        out_specs=vm,
        scratch_shapes=[
            pltpu.VMEM((4 * BLOCKS * ROWS_MSG, 128), F32),
            pltpu.VMEM((TILTS * 2 * BAND, 128), BF),
        ],
        compiler_params=pltpu.CompilerParams(vmem_limit_bytes=VMEM_LIMIT),
        name="project",
    )(recv, start, cst, trig)

    other = pl.pallas_call(
        mate_kernel,
        out_shape=jax.ShapeDtypeStruct((CELLS // 2, 128), BF),
        in_specs=[anym],
        out_specs=anym,
        scratch_shapes=[dma, dma],
        compiler_params=pltpu.CompilerParams(collective_id=2, has_side_effects=True),
        name="mate",
    )(part)

    owners = box_owner[:, 0]
    positions = jnp.arange(owners.shape[0], dtype=jnp.int32)
    earlier = (owners[:, None] == owners[None, :]) & (positions[None, :] < positions[:, None])
    slot_index = jnp.sum(earlier.astype(jnp.int32), axis=1)
    chosen = (owners[None, :] == group) & (slot_index[None, :] == jnp.arange(4, dtype=jnp.int32)[:, None])
    fields = jnp.stack(
        [jnp.ones_like(owners), box_corner[0] - x_block * COLS, box_corner[1], box_corner[2]]
    )
    info = jnp.sum(jnp.where(chosen[:, None, :], fields[None, :, :], 0), axis=2).reshape(16)
    info = jnp.concatenate([info, (group * 32).reshape(1), core.reshape(1)]).astype(jnp.int32)
    boxes, volume = pl.pallas_call(
        box_kernel,
        out_shape=(
            jax.ShapeDtypeStruct((4, BOX, BOX * BOX), BF),
            jax.ShapeDtypeStruct((32, COLS * DEPTH), BF),
        ),
        in_specs=[anym, anym, sm],
        out_specs=(vm, vm),
        scratch_shapes=[pltpu.VMEM((CELLS, 128), BF), dma((2,))],
        compiler_params=pltpu.CompilerParams(vmem_limit_bytes=VMEM_LIMIT),
        name="boxes",
    )(part, other, info)
    return volume.reshape(32, COLS, DEPTH), boxes.reshape(1, 1, 4, BOX, BOX * BOX)


def solution(mesh):
    in_specs = (P("tilt", "vol", None), P("tilt"), P("tilt"), P(None, "vol"), P("vol", None))
    out_specs = (P("tilt", "vol", None), P("vol", "tilt", None, None, None))
    return jax.shard_map(
        per_device, mesh=mesh, in_specs=in_specs, out_specs=out_specs, check_vma=False
    )
```

profile of v0, /device:TPU:1, one launch (start us, length us, event | category | flops | bytes accessed | tf_op | source)
XLA Modules:
  0.0 110.4 jit_solution(16117910884646134681)
XLA Ops:
  0.6 0.7 slice_subtract_fusion
  1.3 0.7 broadcast_compare_fusion
  2.0 0.7 convert_element_type.88
  2.6 0.9 convert_reduce_fusion
  3.6 0.7 slice.33
  4.3 0.1 pad_add_fusion
  4.4 0.1 select_reduce_fusion
  4.5 0.1 reshape.332
  4.6 0.7 pad_add_fusion.1.slot_ref
  5.3 0.7 fusion.14
  6.0 0.7 shift-right-arithmetic_bitcast_fusion
  6.7 0.1 reshape.328
  6.7 0.1 broadcast_in_dim.19
  6.8 0.7 reshape.329.dose_ref
  7.5 0.7 broadcast_in_dim.20.meta_ref
  8.1 0.7 fusion.3
  8.9 1.3 %reshape.326 = bf16[8,2,2,64,64]{4,3,2,1,0:T(8,128)(2,1)S(1)} reshape(bf16[16,2,4096]{2,1,0:T(2,128)(2,1)} %param.9) | data formatting | bytes 524288 | tf_op jit(solution)/shard_map/reshape | solution.py:372
  10.2 0.5 copy.20
  10.7 1.0 reshape.327.x_ref
  11.8 9.1 %filter.1.x_ref = bf16[64,48,128]{2,1,0:T(8,128)(2,1)} custom-call(bf16[8,64,256]{2,1,0:T(8,128)(2,1)} %reshape.327.x_ref, bf16[256,64]{1,0:T(8,128)(2,1)} %constant.105.clone.left_ref, bf16[4,256,256]{2,1,0:T(8,128)(2,1)} %constant.106.clone.right_ref, f32[2,64,128]{2,1,0:T(8,128)} %constant.107.clone.twist_ref, f32[2,64,128]{2,1,0:T(8,128)} %constant.108.clone.shape_ref, ...), custom_call_target="tpu_custom_call" | custom-call | tf_op jit(solution)/shard_map/filter/pallas_call | solution.py:375
  20.9 37.1 %exchange.1.recv_ref = bf16[4,64,48,128]{3,2,1,0:T(8,128)(2,1)} custom-call(bf16[64,48,128]{2,1,0:T(8,128)(2,1)} %filter.1.x_ref), custom_call_target="tpu_custom_call" | custom-call | tf_op jit(solution)/shard_map/exchange/pallas_call | solution.py:386
  58.0 0.8 slice.26
  58.9 0.1 slice_convert_fusion
  59.0 0.2 fusion
  59.2 0.3 cosine_reduce_fusion
  59.5 0.1 reshape.330
  59.6 0.7 multiply_subtract_fusion.start_ref
  60.3 0.1 convert_subtract_fusion
  60.3 0.1 broadcast_in_dim.21
  60.4 0.7 reshape.331.trig_ref
  61.1 0.3 broadcast_subtract_fusion
  61.5 1.0 sub.80.cst_ref
  62.5 26.3 %project.1.x_ref.own_ref = bf16[8192,128]{1,0:T(8,128)(2,1)} custom-call(bf16[4,64,48,128]{3,2,1,0:T(8,128)(2,1)} %exchange.1.recv_ref, s32[32,64]{1,0:T(8,128)} %multiply_subtract_fusion.start_ref, f32[256,256]{1,0:T(8,128)} %sub.80.cst_ref, f32[16,256]{1,0:T(8,128)} %reshape.331.trig_ref), custom_call_target="tpu_custom_call" | custom-call | tf_op jit(solution)/shard_map/project/pallas_call | solution.py:419
  88.8 4.5 %mate.1.other_ref = bf16[8192,128]{1,0:T(8,128)(2,1)} custom-call(bf16[8192,128]{1,0:T(8,128)(2,1)} %project.1.x_ref.own_ref), custom_call_target="tpu_custom_call" | custom-call | tf_op jit(solution)/shard_map/mate/pallas_call | solution.py:432
  93.3 15.1 %boxes.1 = (bf16[4,64,4096]{2,1,0:T(8,128)(2,1)}, bf16[32,8192]{1,0:T(8,128)(2,1)}) custom-call(bf16[8192,128]{1,0:T(8,128)(2,1)} %project.1.x_ref.own_ref, bf16[8192,128]{1,0:T(8,128)(2,1)} %mate.1.other_ref, s32[18]{0:T(128)} %pad_add_fusion.1.slot_ref), custom_call_target="tpu_custom_call" | custom-call | tf_op jit(solution)/shard_map/boxes/pallas_call | solution.py:452
  108.5 2.0 %copy.18 = bf16[4,8,64,128]{3,2,1,0:T(8,128)(2,1)} copy(bf16[4,8,64,128]{3,1,2,0:T(8,128)(2,1)} %bitcast.24) | data formatting | bytes 1048576
  (10 shorter events, 0.1 us)
where the time goes:
time: 112 us; the launch traced here: 110 us
  Pallas kernels  92.2 us (82%)
  local copies, waits for them, and re-layouts  9.85 us (9%)
  other arithmetic  7.64 us (7%)
    pallas_call x1, Pallas kernels, per_device(): pl.pallas_call(exchange_kernel, out_shape=jax.ShapeDtypeStruct((4, BLOCKS...  37.1 us
    pallas_call x1, Pallas kernels, per_device(): pl.pallas_call(project_kernel, out_shape=jax.ShapeDtypeStruct((CELLS // 2...  26.3 us
    pallas_call x1, Pallas kernels, per_device(): pl.pallas_call(box_kernel, out_shape=(jax.ShapeDtypeStruct((4, BOX, BOX *...  15.1 us
    pallas_call x1, Pallas kernels, per_device(): pl.pallas_call(filter_kernel, out_shape=jax.ShapeDtypeStruct((BLOCKS, ROW...  9.13 us
    pallas_call x1, Pallas kernels, per_device(): pl.pallas_call(mate_kernel, out_shape=jax.ShapeDtypeStruct((CELLS // 2, 1...  4.52 us

commit v1 on v0

v1 whole, which is shorter than its diff:
```python
import functools
import math

import jax
import jax.numpy as jnp
import ml_dtypes
import numpy as np
from jax import lax
from jax.experimental import pallas as pl
from jax.experimental.pallas import tpu as pltpu
from jax.sharding import PartitionSpec as P

MESH = pl.DeviceIdType.MESH
BF = jnp.bfloat16
F32 = jnp.float32

PIX = 4096
EDGE = 64
COLS = 64
DEPTH = 128
BOX = 64
BLOCKS = 64
TILTS_HERE = 16
TILTS = 64
ROWS_MSG = 48
BAND = 192
TILE = 16
WIN = 24
LANES = TILTS * WIN
CELLS = 2 * COLS * DEPTH

VMEM_LIMIT = 56 * 1024 * 1024


def split_np(table):
    high = table.astype(np.float32).astype(ml_dtypes.bfloat16)
    low = (table - high.astype(np.float64)).astype(np.float32).astype(ml_dtypes.bfloat16)
    return high, low


def fft_tables():
    grid = np.outer(np.arange(EDGE), np.arange(EDGE))
    cos_t = np.cos(2 * np.pi * (grid % EDGE) / EDGE)
    sin_t = np.sin(2 * np.pi * (grid % EDGE) / EDGE)
    stacked = np.concatenate([cos_t, sin_t], axis=0)
    s_hi, s_lo = split_np(stacked)
    left = np.concatenate([s_hi, s_lo], axis=0)
    order = np.concatenate([np.arange(0, EDGE, 2), np.arange(1, EDGE, 2)])
    left = np.stack([left[:, order], left])
    two = np.eye(2)
    cos2, sin2 = np.kron(two, cos_t), np.kron(two, sin_t)
    fwd = np.block([[cos2, -sin2], [sin2, cos2]])
    inv = np.block([[cos2, sin2], [-sin2, cos2]])
    f_hi, f_lo = split_np(fwd)
    i_hi, i_lo = split_np(inv)
    right = np.stack([f_hi, f_lo, i_hi, i_lo])
    twist = np.stack([np.cos(2 * np.pi * grid / PIX), np.sin(2 * np.pi * grid / PIX)])
    twist = np.concatenate([twist, twist], axis=2).astype(np.float32)
    k1, k2 = np.meshgrid(np.arange(EDGE), np.arange(EDGE), indexing="ij")
    freq = k1 + EDGE * k2
    freq = np.minimum(freq, PIX - freq)
    ratio = 2.0 * freq / PIX
    bend = ratio * np.sqrt(ratio)
    ramp = np.where(freq * 2 == PIX, 0.0, freq / PIX) / PIX
    shape = np.stack([bend, ramp])
    shape = np.concatenate([shape, shape], axis=2).astype(np.float32)
    return left, right, twist, shape


def dot(a, b):
    return jnp.dot(a, b, preferred_element_type=F32)


def dot_t(a, b):
    return lax.dot_general(a, b, (((1,), (1,)), ((), ())), preferred_element_type=F32)


def halves(value):
    high = value.astype(BF)
    return high, (value - high.astype(F32)).astype(BF)


def filter_pairs(pairs, x_ref, left_ref, right_ref, twist_ref, shape_ref, angle_row, angle_ref, dose_ref, cube, scr):
    first_left, left = left_ref[0], left_ref[1]
    cos_w, sin_w = twist_ref[0], twist_ref[1]
    bend, ramp = shape_ref[0], shape_ref[1]
    lane = lax.broadcasted_iota(jnp.int32, (EDGE, 128), 1)
    first = lane < EDGE
    thin = first[0:32]
    n1 = lax.broadcasted_iota(jnp.int32, (BLOCKS, EDGE), 1)
    cosine, sine = trig_of(angle_row[...])
    columns = lax.broadcasted_iota(jnp.int32, (BLOCKS, TILTS_HERE), 0).astype(F32) * COLS
    lowest = (
        PIX / 2
        + (columns - PIX / 2) * cosine
        + jnp.minimum(-(DEPTH / 2) * sine, (DEPTH / 2 - 1) * sine)
    )
    begin = jnp.floor(lowest).astype(jnp.int32) - 1
    quots, rests = begin >> 6, begin & 63

    def side(row, pair):
        one = cube[pl.ds((pair * 4 + row) * 32, 32), :]
        two = cube[pl.ds((pair * 4 + 2 + row) * 32, 32), :]
        even = jnp.where(thin, one, pltpu.roll(two, EDGE, 1))
        odd = jnp.where(thin, pltpu.roll(one, EDGE, 1), two)
        return jnp.concatenate([even, odd], axis=0).astype(BF)

    for pair in pairs:
        part = dot(first_left, jnp.concatenate([side(0, pair), side(1, pair)], axis=1))
        cx = part[0:64] + part[128:192]
        sx = part[64:128] + part[192:256]
        re = cx[:, :128] + sx[:, 128:]
        im = cx[:, 128:] - sx[:, :128]
        turned = jnp.concatenate([re * cos_w + im * sin_w, im * cos_w - re * sin_w], axis=1)
        hi, lo = halves(turned)
        spec = dot(hi, right_ref[0]) + (dot(lo, right_ref[0]) + dot(hi, right_ref[1]))
        dose = jnp.where(first, dose_ref[2 * pair].astype(F32), dose_ref[2 * pair + 1].astype(F32))
        resp = ramp * jnp.exp((-0.05 * dose) * bend)
        spec = spec * jnp.concatenate([resp, resp], axis=1)
        hi, lo = halves(spec)
        back = dot(hi, right_ref[2]) + (dot(lo, right_ref[2]) + dot(hi, right_ref[3]))
        re, im = back[:, :128], back[:, 128:]
        turned = jnp.concatenate([re * cos_w - im * sin_w, im * cos_w + re * sin_w], axis=1)
        hi, lo = halves(turned)
        part = dot(left, hi)
        extra = dot(left[0:128], lo)
        cx = part[0:64] + (part[128:192] + extra[0:64])
        sx = part[64:128] + (part[192:256] + extra[64:128])
        re = cx[:, :128] - sx[:, 128:]
        im = cx[:, 128:] + sx[:, :128]
        rows = (
            jnp.where(first, re, pltpu.roll(im, EDGE, 1)),
            jnp.where(first, pltpu.roll(re, EDGE, 1), im),
        )
        for half in range(2):
            tilt = 2 * pair + half
            image = rows[half].astype(BF)
            quot = quots[:, tilt : tilt + 1]
            rest = rests[:, tilt : tilt + 1]
            pick = jnp.concatenate(
                [(n1 == quot + step).astype(F32).astype(BF) for step in range(4)], axis=0
            )
            near = dot(pick, image)
            at = (lane & EDGE) | ((lane + rest) & (EDGE - 1))
            stay = (lane & (EDGE - 1)) + rest < EDGE
            moved = [
                jnp.take_along_axis(near[step * EDGE : (step + 1) * EDGE], at, axis=1)
                for step in range(4)
            ]
            for step in range(3):
                piece = jnp.where(stay, moved[step], moved[step + 1])
                if step == 2:
                    tenths = angle_ref[tilt]
                    piece = jnp.where(lane == 60, (tenths >> 5).astype(F32), piece)
                    piece = jnp.where(lane == 61, (tenths & 31).astype(F32), piece)
                    piece = jnp.where(lane == 62, quot.astype(F32), piece)
                    piece = jnp.where(lane == 63, rest.astype(F32), piece)
                scr[pl.ds(tilt * 3 + step, BLOCKS, stride=ROWS_MSG), :] = piece


def exchange_kernel(
    image_ref, left_ref, right_ref, twist_ref, shape_ref, angle_row, angle_ref, dose_ref, o_ref,
    cube, scr, x_ref, loc_sem, a_send, a_recv, x_send, x_recv, m_send, m_recv,
):
    v = lax.axis_index("vol")
    t = lax.axis_index("tilt")
    y, z, xh = lax.rem(v, 4), lax.rem(v // 4, 8), v // 32
    core, xl = lax.rem(t, 2), t // 2
    mate = xl * 2 + (1 - core)
    cross = (1 - xl) * 2 + core
    barrier = pltpu.get_barrier_semaphore()

    def greet(i, carry):
        p = lax.rem(xh * 32 + i, 64)
        q = jnp.where(i < 32, t, cross)

        @pl.when(p != v)
        def _():
            pl.semaphore_signal(barrier, inc=1, device_id=(p, q), device_id_type=MESH)

        return carry

    lax.fori_loop(0, 64, greet, 0)
    pl.semaphore_signal(barrier, inc=1, device_id=(v, cross), device_id_type=MESH)
    pl.semaphore_signal(barrier, inc=1, device_id=(v, mate), device_id_type=MESH)

    for tilt in range(TILTS_HERE):
        wide = image_ref[tilt].astype(F32)
        for j in range(PIX // 128):
            cube[pl.ds(tilt * 64 + j, 2, stride=32), :] = wide[:, j * 128 : (j + 1) * 128]

    operands = (image_ref, left_ref, right_ref, twist_ref, shape_ref, angle_row, angle_ref, dose_ref, cube, scr)
    steps = (0, 1, 7, 2, 6, 3, 5, 4)

    def send_rows(low, high):
        for block in range(BLOCKS):
            x_ref[block, low:high] = scr[block * ROWS_MSG + low : block * ROWS_MSG + high, :].astype(BF)
        for dz in steps:
            for far in range(2):
                for dy in range(4):
                    if dz == 0 and far == 0 and dy == 0:
                        continue
                    zz, yy = lax.rem(z + dz, 8), lax.rem(y + dy, 4)
                    p = (xh if far == 0 else 1 - xh) * 32 + zz * 4 + yy
                    pltpu.make_async_remote_copy(
                        x_ref.at[p, pl.ds(low, high - low)],
                        o_ref.at[t, v, pl.ds(low, high - low)],
                        a_send,
                        a_recv.at[far, z],
                        device_id=(p, t if far == 0 else cross),
                        device_id_type=MESH,
                    ).start()

    filter_pairs(range(0, 3), *operands)
    pl.semaphore_wait(barrier, 65)
    send_rows(0, 16)
    filter_pairs(range(3, 8), *operands)
    send_rows(16, 48)
    own = pltpu.make_async_copy(x_ref.at[v], o_ref.at[t, v], loc_sem)
    own.start()
    for dz in steps:
        for far in range(2):
            zz = lax.rem(z + 8 - dz, 8)
            base = (xh if far == 0 else 1 - xh) * 32 + zz * 4
            slot = t if far == 0 else cross
            number = 4
            if dz == 0 and far == 0:
                own.wait()
                number = 3
            pltpu.make_async_copy(
                o_ref.at[slot, pl.ds(base, number)], o_ref.at[slot, pl.ds(base, number)], a_recv.at[far, zz]
            ).wait()
            block = o_ref.at[slot, pl.ds(base, 4)]
            pltpu.make_async_remote_copy(
                block, block, x_send, x_recv.at[far, zz], device_id=(v, cross), device_id_type=MESH
            ).start()
            pltpu.make_async_remote_copy(
                block, block, m_send, m_recv.at[0, far, zz], device_id=(v, mate), device_id_type=MESH
            ).start()
    for dz in steps:
        for far in range(2):
            zz = lax.rem(z + 8 - dz, 8)
            base = (xh if far == 0 else 1 - xh) * 32 + zz * 4
            slot = cross if far == 0 else t
            block = o_ref.at[slot, pl.ds(base, 4)]
            pltpu.make_async_copy(block, block, x_recv.at[far, zz]).wait()
            pltpu.make_async_remote_copy(
                block, block, m_send, m_recv.at[1, far, zz], device_id=(v, mate), device_id_type=MESH
            ).start()
    mate_cross = (1 - xl) * 2 + (1 - core)
    for kind in range(2):
        for far in range(2):
            for zz in range(8):
                base = (xh if far == 0 else 1 - xh) * 32 + zz * 4
                slot = mate if (kind + far) % 2 == 0 else mate_cross
                block = o_ref.at[slot, pl.ds(base, 4)]
                pltpu.make_async_copy(block, block, m_recv.at[kind, far, zz]).wait()
    pltpu.make_async_copy(x_ref.at[pl.ds(0, 63)], x_ref.at[pl.ds(0, 63)], a_send).wait()
    half = o_ref.at[0]
    pltpu.make_async_copy(half, half, x_send).wait()
    both = o_ref.at[pl.ds(0, 2)]
    pltpu.make_async_copy(both, both, m_send).wait()


def project_kernel(recv_ref, lane_tilt, lane_pixel, part, land, scr, win, starts_v, starts_s, cst, trig, sem, sem2):
    v = lax.axis_index("vol")
    core = lax.rem(lax.axis_index("tilt"), 2)
    size = BLOCKS * ROWS_MSG
    arrive = [pltpu.make_async_copy(recv_ref.at[g], land.at[g], sem.at[g]) for g in range(4)]
    for copy in arrive:
        copy.start()
    lane = lax.broadcasted_iota(jnp.int32, (BLOCKS, 128), 1)
    low = lane < EDGE
    fold = (
        lax.broadcasted_iota(jnp.int32, (EDGE, 128), 0) == (lane & (EDGE - 1))
    ).astype(F32).astype(BF)
    for group in range(4):
        arrive[group].wait()
        scr[group * size : (group + 1) * size, :] = land[group].reshape(size, 128).astype(F32)

    heads = [scr[pl.ds(g * size + 2, TILTS_HERE, stride=3), :] for g in range(4)]
    heads = jnp.concatenate(heads + [jnp.zeros((128 - TILTS, 128), F32)], axis=0).T
    tenths = heads[60:61] * 32.0 + heads[61:62]
    base = heads[62:63] * 64.0 + heads[63:64]
    cosine, sine = trig_of(tenths)
    number = lax.broadcasted_iota(jnp.int32, (32, 128), 0)
    x_tile = ((number >> 3) * TILE + (v + core) * COLS).astype(F32)
    z_tile = ((number & 7) * TILE).astype(F32)
    coord = PIX / 2 + (x_tile - PIX / 2) * cosine + (z_tile - DEPTH / 2) * sine
    local = jnp.floor(coord + jnp.minimum((TILE - 1) * sine, 0.0)) - base
    local = jnp.clip(local, 0.0, float(BAND - 8 - WIN))
    tilt_lane = jnp.minimum(lax.broadcasted_iota(jnp.int32, (32, 128), 1), TILTS - 1)
    starts_v[...] = tilt_lane * BAND + local.astype(jnp.int32)
    to_smem = pltpu.make_async_copy(starts_v, starts_s, sem2)
    to_smem.start()
    offset = coord - (base + local)
    both = jnp.concatenate([jnp.broadcast_to(cosine, (8, 128)), jnp.broadcast_to(sine, (8, 128))], axis=0)
    for g in range(LANES // 128):
        lanes = slice(g * 128, (g + 1) * 128)
        which = jnp.broadcast_to(lane_tilt[0:1, lanes], (32, 128))
        cst[:, lanes] = jnp.take_along_axis(offset, which, axis=1) - lane_pixel[0:1, lanes]
        trig[:, lanes] = jnp.take_along_axis(both, which[0:16], axis=1)

    batch = 16

    def turn(group, carry):
        wide = []
        for b in range(batch):
            for step in range(3):
                piece = scr[pl.ds(group * size + b * 3 + step, BLOCKS, stride=ROWS_MSG), :]
                wide += [jnp.where(low, piece, 0.0).astype(BF), jnp.where(low, 0.0, piece).astype(BF)]
        turned = dot_t(fold, jnp.concatenate(wide, axis=0))
        for i in range(3 * batch):
            at = pl.multiple_of(group * (batch * BAND) + i * EDGE, EDGE)
            win[pl.ds(at, EDGE), :] = turned[:, i * 128 : (i + 1) * 128]
        return carry

    lax.fori_loop(0, 4, turn, 0)
    to_smem.wait()

    zcol = lax.broadcasted_iota(jnp.int32, (TILE, 256), 0).astype(F32)

    def tile(number, carry):
        right = jnp.concatenate(
            [win[pl.ds(starts_s[number, i], WIN), :] for i in range(TILTS)], axis=0
        ).astype(BF)
        total = jnp.zeros((TILE * TILE, 128), F32)
        for chunk in range(LANES // 256):
            lanes = slice(chunk * 256, (chunk + 1) * 256)
            cos_l = trig[0:1, lanes]
            here = zcol * trig[8:9, lanes] + cst[pl.ds(number, 1), lanes]
            pieces = []
            for _ in range(TILE):
                pieces.append(jnp.maximum(1.0 - jnp.abs(here), 0.0).astype(BF))
                here = here + cos_l
            total = total + dot(jnp.concatenate(pieces, axis=0), right[lanes])
        rounded = total.astype(BF)
        xt, zt = number // 8, lax.rem(number, 8)
        for i in range(TILE):
            at = pl.multiple_of((xt * TILE + i) * DEPTH + zt * TILE, TILE)
            part[pl.ds(at, TILE), :] = rounded[i * TILE : (i + 1) * TILE]
        return carry

    lax.fori_loop(0, 32, tile, 0)


def mate_kernel(x_ref, o_ref, send, recv):
    v = lax.axis_index("vol")
    t = lax.axis_index("tilt")
    mate = (t // 2) * 2 + (1 - lax.rem(t, 2))
    barrier = pltpu.get_barrier_semaphore()
    pl.semaphore_signal(barrier, inc=1, device_id=(v, mate), device_id_type=MESH)
    pl.semaphore_wait(barrier, 1)
    there = pltpu.make_async_remote_copy(
        x_ref, o_ref, send, recv, device_id=(v, mate), device_id_type=MESH
    )
    there.start()
    there.wait()


def box_kernel(own_ref, other_ref, corner_ref, owner_ref, box_out, vol_out, land, ext, lines, box_ref, vol_ref, sem, out_sem):
    v = lax.axis_index("vol")
    t = lax.axis_index("tilt")
    core = lax.rem(t, 2)
    half = CELLS // 2
    arrive = [
        pltpu.make_async_copy(own_ref, land.at[core], sem.at[0]),
        pltpu.make_async_copy(other_ref, land.at[1 - core], sem.at[1]),
    ]
    for copy in arrive:
        copy.start()
    picks = owner_ref.shape[0]
    owners = [owner_ref[r, 0] for r in range(picks)]
    ranks = [sum([(owners[q] == owners[r]).astype(jnp.int32) for q in range(r)], jnp.int32(0)) for r in range(picks)]
    lane = lax.broadcasted_iota(jnp.int32, (BOX, 128), 1)
    y_of = (lane & 63) * 2 + (lane >> 6)
    line = lax.broadcasted_iota(jnp.int32, (BOX, 128), 0)
    quarter = (y_of == line + t * 32).astype(F32).astype(BF)[0:32]
    for copy in arrive:
        copy.wait()

    def slab(i, carry):
        rows = land[0, pl.ds(pl.multiple_of(i * 1024, 1024), 1024), :]
        both = dot_t(quarter, rows)
        for j in range(8):
            lines[pl.ds(i * 8 + j, 32, stride=COLS), :] = both[:, j * 128 : (j + 1) * 128]
        return carry

    lax.fori_loop(0, COLS // 8, slab, 0, unroll=2)
    for i in range(32):
        vol_ref[i] = lines[i * COLS : (i + 1) * COLS, :].astype(BF)
    copies = [pltpu.make_async_copy(vol_ref, vol_out, out_sem.at[4])]
    copies[0].start()
    for side in range(2):
        for i in range(8):
            ext[side * half + i * 1024 : side * half + (i + 1) * 1024, :] = land[
                side, i * 1024 : (i + 1) * 1024
            ].astype(F32)

    for slot in range(4):
        mine = [((owners[r] == t) & (ranks[r] == slot)).astype(jnp.int32) for r in range(picks)]
        present = sum(mine)
        x0 = sum([mine[r] * (corner_ref[0, r] - v * COLS) for r in range(picks)])
        y0 = sum([mine[r] * corner_ref[1, r] for r in range(picks)])
        z0 = sum([mine[r] * corner_ref[2, r] for r in range(picks)])
        chosen = ((y_of == line + y0) & (present > 0)).astype(F32).astype(BF)
        origin = x0 * DEPTH + z0

        def cut(i, carry):
            rows = jnp.concatenate(
                [ext[pl.ds(origin + (i * 8 + j) * DEPTH, BOX), :] for j in range(8)], axis=0
            ).astype(BF)
            box_ref[slot, :, pl.ds(pl.multiple_of(i * 512, 512), 512)] = dot_t(chosen, rows).astype(BF)
            return carry

        lax.fori_loop(0, BOX // 8, cut, 0, unroll=2)
        copies.append(pltpu.make_async_copy(box_ref.at[slot], box_out.at[slot], out_sem.at[slot]))
        copies[-1].start()
    for copy in copies:
        copy.wait()


def trig_of(tenths):
    angle = tenths.astype(F32) * (math.pi / 1800.0)
    return jnp.cos(angle), jnp.sin(angle)


def per_device(images, angle_tenths, dose_index, box_corner, box_owner):
    vm = pl.BlockSpec(memory_space=pltpu.VMEM)
    sm = pl.BlockSpec(memory_space=pltpu.SMEM)
    anym = pl.BlockSpec(memory_space=pl.ANY)
    dma = pltpu.SemaphoreType.DMA
    tables = [jnp.asarray(a) for a in fft_tables()]
    recv = pl.pallas_call(
        exchange_kernel,
        out_shape=jax.ShapeDtypeStruct((4, BLOCKS, ROWS_MSG, 128), BF),
        in_specs=[vm] * 6 + [sm] * 2,
        out_specs=anym,
        scratch_shapes=[
            pltpu.VMEM((32 * 32, 128), F32),
            pltpu.VMEM((BLOCKS * ROWS_MSG, 128), F32),
            pltpu.VMEM((BLOCKS, ROWS_MSG, 128), BF),
            dma, dma, dma((2, 8)), dma, dma((2, 8)), dma, dma((2, 2, 8)),
        ],
        compiler_params=pltpu.CompilerParams(
            vmem_limit_bytes=VMEM_LIMIT, collective_id=1, has_side_effects=True
        ),
        name="exchange",
    )(images, *tables, angle_tenths.reshape(1, TILTS_HERE), angle_tenths, dose_index)

    lanes = np.arange(LANES)
    lane_tilt = jnp.asarray(np.broadcast_to(lanes // WIN, (8, LANES)).astype(np.int32))
    lane_pixel = jnp.asarray(np.broadcast_to(lanes % WIN, (8, LANES)).astype(np.float32))
    part = pl.pallas_call(
        project_kernel,
        out_shape=jax.ShapeDtypeStruct((CELLS // 2, 128), BF),
        in_specs=[anym, vm, vm],
        out_specs=vm,
        scratch_shapes=[
            pltpu.VMEM((4, BLOCKS, ROWS_MSG, 128), BF),
            pltpu.VMEM((4 * BLOCKS * ROWS_MSG, 128), F32),
            pltpu.VMEM((TILTS * BAND, 128), F32),
            pltpu.VMEM((32, 128), jnp.int32),
            pltpu.SMEM((32, 128), jnp.int32),
            pltpu.VMEM((32, LANES), F32),
            pltpu.VMEM((16, LANES), F32),
            dma((4,)),
            dma,
        ],
        compiler_params=pltpu.CompilerParams(vmem_limit_bytes=VMEM_LIMIT),
        name="project",
    )(recv, lane_tilt, lane_pixel)

    other = pl.pallas_call(
        mate_kernel,
        out_shape=jax.ShapeDtypeStruct((CELLS // 2, 128), BF),
        in_specs=[anym],
        out_specs=anym,
        scratch_shapes=[dma, dma],
        compiler_params=pltpu.CompilerParams(collective_id=2, has_side_effects=True),
        name="mate",
    )(part)

    boxes, volume = pl.pallas_call(
        box_kernel,
        out_shape=(
            jax.ShapeDtypeStruct((4, BOX, BOX * BOX), BF),
            jax.ShapeDtypeStruct((32, COLS, DEPTH), BF),
        ),
        in_specs=[anym, anym, sm, sm],
        out_specs=(anym, anym),
        scratch_shapes=[
            pltpu.VMEM((2, CELLS // 2, 128), BF),
            pltpu.VMEM((CELLS, 128), F32),
            pltpu.VMEM((32 * COLS, 128), F32),
            pltpu.VMEM((4, BOX, BOX * BOX), BF),
            pltpu.VMEM((32, COLS, DEPTH), BF),
            dma((2,)),
            dma((5,)),
        ],
        compiler_params=pltpu.CompilerParams(vmem_limit_bytes=VMEM_LIMIT),
        name="boxes",
    )(part, other, box_corner, box_owner)
    return volume, boxes.reshape(1, 1, 4, BOX, BOX * BOX)


def solution(mesh):
    in_specs = (P("tilt", "vol", None), P("tilt"), P("tilt"), P(None, "vol"), P("vol", None))
    out_specs = (P("tilt", "vol", None), P("vol", "tilt", None, None, None))
    return jax.shard_map(
        per_device, mesh=mesh, in_specs=in_specs, out_specs=out_specs, check_vma=False
    )
```

time: 112 us -> 81.3 us (0.73); the launches traced: 110 us -> 81.1 us
  Pallas kernels: 92.2 us -> 79.1 us
  local copies, waits for them, and re-layouts: 9.85 us -> 1.32 us
  other arithmetic: 7.64 us -> 0 us
    pallas_call x1 -> x0, Pallas kernels: 9.13 us -> none  [per_device(): pl.pallas_call(filter_kernel, out_shape=jax.ShapeDtypeStruct((BLOCKS, ROW...]
    pallas_call x1, Pallas kernels: 37.1 us -> 44 us  [per_device(): pl.pallas_call(exchange_kernel, out_shape=jax.ShapeDtypeStruct((4, BLOCKS...]
    pallas_call x1, Pallas kernels: 15.1 us -> 9.24 us  [per_device(): pl.pallas_call(box_kernel, out_shape=(jax.ShapeDtypeStruct((4, BOX, BOX *...]
    pallas_call x1, Pallas kernels: 26.3 us -> 21.2 us  [per_device(): pl.pallas_call(project_kernel, out_shape=jax.ShapeDtypeStruct((CELLS // 2...]
    reshape x8 -> x0, local copies, waits for them, and re-layouts: 4.53 us -> none  [the longest x2 1.87 us: per_device(): images.reshape(TILTS_HERE // 2, 2, 2, EDGE, EDGE).transpose(0, 3, 2, 1, 4)]
    sub x6 -> x0, other arithmetic: 1.82 us -> none  [the longest x1 0.7 us: per_device(): start = (tilt_number * 2 + odd) * BAND + local8 - 8 * odd]
    slice x2 -> x0, local copies, waits for them, and re-layouts: 1.49 us -> none  [the longest x1 0.81 us: per_device(): heads = recv[:, 0].reshape(TILTS, 3, 128)[:, 2, 60:64].astype(jnp.int32)]
where the time goes in v1:
time: 81.3 us; the launch traced here: 81.1 us
  Pallas kernels  79.1 us (97%)
  local copies, waits for them, and re-layouts  1.32 us (2%)
    pallas_call x1, Pallas kernels, per_device(): pl.pallas_call(exchange_kernel, out_shape=jax.ShapeDtypeStruct((4, BLOCKS...  44 us
    pallas_call x1, Pallas kernels, per_device(): pl.pallas_call(project_kernel, out_shape=jax.ShapeDtypeStruct((CELLS // 2...  21.2 us
    pallas_call x1, Pallas kernels, per_device(): pl.pallas_call(box_kernel, out_shape=(jax.ShapeDtypeStruct((4, BOX, BOX *...  9.24 us
    pallas_call x1, Pallas kernels, per_device(): pl.pallas_call(mate_kernel, out_shape=jax.ShapeDtypeStruct((CELLS // 2, 1...  4.68 us

profile of v1, /device:TPU:1, one launch (start us, length us, event | category | flops | bytes accessed | tf_op | source)
XLA Modules:
  0.0 81.1 jit_solution(1176605595350617985)
XLA Ops:
  0.6 1.3 %copy.13.owner_ref = s32[8,1]{1,0:T(8,128)} copy(s32[8,1]{0,1:T(1,128)} %param.15) | data formatting | bytes 64 | tf_op args[4]
  2.0 44.0 %exchange.1.recv_ref = bf16[4,64,48,128]{3,2,1,0:T(8,128)(2,1)} custom-call(bf16[16,2,4096]{2,1,0:T(2,128)(2,1)} %image_ref.1, bf16[2,256,64]{2,1,0:T(8,128)(2,1)} %constant.12.clone.left_ref, bf16[4,256,256]{2,1,0:T(8,128)(2,1)} %constant.13.clone.right_ref, f32[2,64,128]{2,1,0:T(8,128)} %constant.14.clone.twist_ref, ...), custom_call_target="tpu_custom_call" | custom-call | tf_op jit(solution)/shard_map/exchange/pallas_call | solution.py:434
  45.9 21.2 %project.1.x_ref.own_ref = bf16[8192,128]{1,0:T(8,128)(2,1)} custom-call(bf16[4,64,48,128]{3,2,1,0:T(8,128)(2,1)} %exchange.1.recv_ref, s32[8,1536]{1,0:T(8,128)} %constant.16.clone.lane_tilt, f32[8,1536]{1,0:T(8,128)} %constant.17.clone.lane_pixel), custom_call_target="tpu_custom_call" | custom-call | tf_op jit(solution)/shard_map/project/pallas_call | solution.py:454
  67.2 4.7 %mate.1.other_ref = bf16[8192,128]{1,0:T(8,128)(2,1)} custom-call(bf16[8192,128]{1,0:T(8,128)(2,1)} %project.1.x_ref.own_ref), custom_call_target="tpu_custom_call" | custom-call | tf_op jit(solution)/shard_map/mate/pallas_call | solution.py:474
  71.8 9.2 %boxes.1 = (bf16[4,64,4096]{2,1,0:T(8,128)(2,1)}, bf16[32,64,128]{2,1,0:T(8,128)(2,1)}) custom-call(bf16[8192,128]{1,0:T(8,128)(2,1)} %project.1.x_ref.own_ref, bf16[8192,128]{1,0:T(8,128)(2,1)} %mate.1.other_ref, s32[3,8]{1,0:T(4,128)} %corner_ref.1, s32[8,1]{1,0:T(8,128)} %copy.13.owner_ref), custom_call_target="tpu_custom_call" | custom-call | tf_op jit(solution)/shard_map/boxes/pallas_call | solution.py:484

commit v2 on v1

--- a/solution.py
+++ b/solution.py
@@ -262,9 +262,16 @@
     pltpu.make_async_copy(both, both, m_send).wait()
 
 
-def project_kernel(recv_ref, lane_tilt, lane_pixel, part, land, scr, win, starts_v, starts_s, cst, trig, sem, sem2):
+def project_kernel(
+    recv_ref, lane_tilt, lane_pixel, own_ref, other_ref,
+    land, scr, win, starts_v, starts_s, cst, trig, part, sem, sem2, loc, send, recv,
+):
     v = lax.axis_index("vol")
-    core = lax.rem(lax.axis_index("tilt"), 2)
+    t = lax.axis_index("tilt")
+    core = lax.rem(t, 2)
+    mate = (t // 2) * 2 + (1 - core)
+    barrier = pltpu.get_barrier_semaphore()
+    pl.semaphore_signal(barrier, inc=1, device_id=(v, mate), device_id_type=MESH)
     size = BLOCKS * ROWS_MSG
     arrive = [pltpu.make_async_copy(recv_ref.at[g], land.at[g], sem.at[g]) for g in range(4)]
     for copy in arrive:
@@ -288,12 +295,12 @@
     z_tile = ((number & 7) * TILE).astype(F32)
     coord = PIX / 2 + (x_tile - PIX / 2) * cosine + (z_tile - DEPTH / 2) * sine
     local = jnp.floor(coord + jnp.minimum((TILE - 1) * sine, 0.0)) - base
-    local = jnp.clip(local, 0.0, float(BAND - 8 - WIN))
+    local = jnp.clip(local.astype(jnp.int32), 0, BAND - 8 - WIN)
     tilt_lane = jnp.minimum(lax.broadcasted_iota(jnp.int32, (32, 128), 1), TILTS - 1)
-    starts_v[...] = tilt_lane * BAND + local.astype(jnp.int32)
+    starts_v[...] = tilt_lane * BAND + local
     to_smem = pltpu.make_async_copy(starts_v, starts_s, sem2)
     to_smem.start()
-    offset = coord - (base + local)
+    offset = coord - (base + local.astype(F32))
     both = jnp.concatenate([jnp.broadcast_to(cosine, (8, 128)), jnp.broadcast_to(sine, (8, 128))], axis=0)
     for g in range(LANES // 128):
         lanes = slice(g * 128, (g + 1) * 128)
@@ -341,21 +348,23 @@
             part[pl.ds(at, TILE), :] = rounded[i * TILE : (i + 1) * TILE]
         return carry
 
-    lax.fori_loop(0, 32, tile, 0)
-
-
-def mate_kernel(x_ref, o_ref, send, recv):
-    v = lax.axis_index("vol")
-    t = lax.axis_index("tilt")
-    mate = (t // 2) * 2 + (1 - lax.rem(t, 2))
-    barrier = pltpu.get_barrier_semaphore()
-    pl.semaphore_signal(barrier, inc=1, device_id=(v, mate), device_id_type=MESH)
-    pl.semaphore_wait(barrier, 1)
-    there = pltpu.make_async_remote_copy(
-        x_ref, o_ref, send, recv, device_id=(v, mate), device_id_type=MESH
-    )
-    there.start()
-    there.wait()
+    span = TILE * DEPTH
+    copies = []
+    for xt in range(4):
+        lax.fori_loop(8 * xt, 8 * xt + 8, tile, 0)
+        if xt == 0:
+            pl.semaphore_wait(barrier, 1)
+        slab = pl.ds(xt * span, span)
+        there = pltpu.make_async_remote_copy(
+            part.at[slab], other_ref.at[slab], send.at[xt], recv.at[xt],
+            device_id=(v, mate), device_id_type=MESH,
+        )
+        here = pltpu.make_async_copy(part.at[slab], own_ref.at[slab], loc.at[xt])
+        there.start()
+        here.start()
+        copies += [there, here]
+    for copy in copies:
+        copy.wait()
 
 
 def box_kernel(own_ref, other_ref, corner_ref, owner_ref, box_out, vol_out, land, ext, lines, box_ref, vol_ref, sem, out_sem):
@@ -369,8 +378,8 @@
     ]
     for copy in arrive:
         copy.start()
-    picks = owner_ref.shape[0]
-    owners = [owner_ref[r, 0] for r in range(picks)]
+    picks = owner_ref.shape[1]
+    owners = [owner_ref[0, r] for r in range(picks)]
     ranks = [sum([(owners[q] == owners[r]).astype(jnp.int32) for q in range(r)], jnp.int32(0)) for r in range(picks)]
     lane = lax.broadcasted_iota(jnp.int32, (BOX, 128), 1)
     y_of = (lane & 63) * 2 + (lane >> 6)
@@ -451,11 +460,11 @@
     lanes = np.arange(LANES)
     lane_tilt = jnp.asarray(np.broadcast_to(lanes // WIN, (8, LANES)).astype(np.int32))
     lane_pixel = jnp.asarray(np.broadcast_to(lanes % WIN, (8, LANES)).astype(np.float32))
-    part = pl.pallas_call(
+    part, other = pl.pallas_call(
         project_kernel,
-        out_shape=jax.ShapeDtypeStruct((CELLS // 2, 128), BF),
+        out_shape=(jax.ShapeDtypeStruct((CELLS // 2, 128), BF),) * 2,
         in_specs=[anym, vm, vm],
-        out_specs=vm,
+        out_specs=(anym, anym),
         scratch_shapes=[
             pltpu.VMEM((4, BLOCKS, ROWS_MSG, 128), BF),
             pltpu.VMEM((4 * BLOCKS * ROWS_MSG, 128), F32),
@@ -464,22 +473,18 @@
             pltpu.SMEM((32, 128), jnp.int32),
             pltpu.VMEM((32, LANES), F32),
             pltpu.VMEM((16, LANES), F32),
+            pltpu.VMEM((CELLS // 2, 128), BF),
             dma((4,)),
             dma,
+            dma((4,)),
+            dma((4,)),
+            dma((4,)),
         ],
-        compiler_params=pltpu.CompilerParams(vmem_limit_bytes=VMEM_LIMIT),
+        compiler_params=pltpu.CompilerParams(
+            vmem_limit_bytes=VMEM_LIMIT, collective_id=2, has_side_effects=True
+        ),
         name="project",
     )(recv, lane_tilt, lane_pixel)
-
-    other = pl.pallas_call(
-        mate_kernel,
-        out_shape=jax.ShapeDtypeStruct((CELLS // 2, 128), BF),
-        in_specs=[anym],
-        out_specs=anym,
-        scratch_shapes=[dma, dma],
-        compiler_params=pltpu.CompilerParams(collective_id=2, has_side_effects=True),
-        name="mate",
-    )(part)
 
     boxes, volume = pl.pallas_call(
         box_kernel,
@@ -500,7 +505,7 @@
         ],
         compiler_params=pltpu.CompilerParams(vmem_limit_bytes=VMEM_LIMIT),
         name="boxes",
-    )(part, other, box_corner, box_owner)
+    )(part, other, box_corner, box_owner.T)
     return volume, boxes.reshape(1, 1, 4, BOX, BOX * BOX)
 
 

time: 81.3 us -> 75.9 us (0.934)
  Pallas kernels: 79.1 us -> 75.1 us
  local copies, waits for them, and re-layouts: 1.32 us -> 0 us
    pallas_call x2 -> x1, Pallas kernels: 25.9 us -> 21.8 us  [per_device(): pl.pallas_call(project_kernel, out_shape=(jax.ShapeDtypeStruct((CELLS //...]
    unnamed x1 -> x0, local copies, waits for them, and re-layouts: 1.32 us -> none
where the time goes in v2:
time: 75.9 us; the launch traced here: 75.7 us
  Pallas kernels  75.1 us (99%)
    pallas_call x1, Pallas kernels, per_device(): pl.pallas_call(exchange_kernel, out_shape=jax.ShapeDtypeStruct((4, BLOCKS...  44.1 us
    pallas_call x1, Pallas kernels, per_device(): pl.pallas_call(project_kernel, out_shape=(jax.ShapeDtypeStruct((CELLS //...  21.8 us
    pallas_call x1, Pallas kernels, per_device(): pl.pallas_call(box_kernel, out_shape=(jax.ShapeDtypeStruct((4, BOX, BOX *...  9.18 us

profile of v2, /device:TPU:1, one launch (start us, length us, event | category | flops | bytes accessed | tf_op | source)
XLA Modules:
  0.0 75.7 jit_solution(7015742957906023871)
XLA Ops:
  0.6 44.1 %exchange.1.recv_ref = bf16[4,64,48,128]{3,2,1,0:T(8,128)(2,1)} custom-call(bf16[16,2,4096]{2,1,0:T(2,128)(2,1)} %image_ref.1, bf16[2,256,64]{2,1,0:T(8,128)(2,1)} %constant.12.clone.left_ref, bf16[4,256,256]{2,1,0:T(8,128)(2,1)} %constant.13.clone.right_ref, f32[2,64,128]{2,1,0:T(8,128)} %constant.14.clone.twist_ref, ...), custom_call_target="tpu_custom_call" | custom-call | tf_op jit(solution)/shard_map/exchange/pallas_call | solution.py:443
  44.7 21.8 %project.1 = (bf16[8192,128]{1,0:T(8,128)(2,1)}, bf16[8192,128]{1,0:T(8,128)(2,1)}) custom-call(bf16[4,64,48,128]{3,2,1,0:T(8,128)(2,1)} %exchange.1.recv_ref, s32[8,1536]{1,0:T(8,128)} %constant.16.clone.lane_tilt, f32[8,1536]{1,0:T(8,128)} %constant.17.clone.lane_pixel), custom_call_target="tpu_custom_call" | custom-call | tf_op jit(solution)/shard_map/project/pallas_call | solution.py:463
  66.5 9.2 %boxes.1 = (bf16[4,64,4096]{2,1,0:T(8,128)(2,1)}, bf16[32,64,128]{2,1,0:T(8,128)(2,1)}) custom-call(bf16[8192,128]{1,0:T(8,128)(2,1)} %get-tuple-element.6.own_ref, bf16[8192,128]{1,0:T(8,128)(2,1)} %get-tuple-element.7.other_ref, s32[3,8]{1,0:T(4,128)} %corner_ref.1, s32[1,8]{1,0:T(1,128)} %bitcast.4), custom_call_target="tpu_custom_call" | custom-call | tf_op jit(solution)/shard_map/boxes/pallas_call | solution.py:489

commit v3 on v2

--- a/solution.py
+++ b/solution.py
@@ -22,11 +22,15 @@
 BLOCKS = 64
 TILTS_HERE = 16
 TILTS = 64
-ROWS_MSG = 48
 BAND = 192
 TILE = 16
 WIN = 24
-LANES = TILTS * WIN
+STAGE_ROWS = 16
+SPLIT = 5
+STAGE_TILTS = ((0, 1, 2, 3, 4), (6, 7, 8, 9, 10), (11, 12, 13, 14, 15, SPLIT))
+STAGE_CHUNKS = ((256, 256), (256, 256), (256, 256, 128))
+STAGE_LANES = (0, 512, 1024, 1792)
+META = 56
 CELLS = 2 * COLS * DEPTH
 
 VMEM_LIMIT = 56 * 1024 * 1024
@@ -78,6 +82,13 @@
 def halves(value):
     high = value.astype(BF)
     return high, (value - high.astype(F32)).astype(BF)
+
+
+def message_row(tilt, step):
+    if tilt == SPLIT:
+        return step, STAGE_ROWS - 1
+    order = tilt - (tilt > SPLIT)
+    return order // 5, 3 * (order % 5) + step
 
 
 def filter_pairs(pairs, x_ref, left_ref, right_ref, twist_ref, shape_ref, angle_row, angle_ref, dose_ref, cube, scr):
@@ -149,18 +160,26 @@
             ]
             for step in range(3):
                 piece = jnp.where(stay, moved[step], moved[step + 1])
-                if step == 2:
-                    tenths = angle_ref[tilt]
-                    piece = jnp.where(lane == 60, (tenths >> 5).astype(F32), piece)
-                    piece = jnp.where(lane == 61, (tenths & 31).astype(F32), piece)
-                    piece = jnp.where(lane == 62, quot.astype(F32), piece)
-                    piece = jnp.where(lane == 63, rest.astype(F32), piece)
-                scr[pl.ds(tilt * 3 + step, BLOCKS, stride=ROWS_MSG), :] = piece
-
-
-def exchange_kernel(
-    image_ref, left_ref, right_ref, twist_ref, shape_ref, angle_row, angle_ref, dose_ref, o_ref,
-    cube, scr, x_ref, loc_sem, a_send, a_recv, x_send, x_recv, m_send, m_recv,
+                if step == 2 and tilt < 4:
+                    for j in range(4):
+                        other = 4 * tilt + j
+                        tenths = angle_ref[other]
+                        at_lane = META + 2 * j
+                        piece = jnp.where(lane == at_lane, (tenths >> 5).astype(F32), piece)
+                        piece = jnp.where(lane == at_lane + 1, (tenths & 31).astype(F32), piece)
+                        quot_o = quots[:, other : other + 1].astype(F32)
+                        rest_o = rests[:, other : other + 1].astype(F32)
+                        piece = jnp.where(lane == at_lane + 64, quot_o, piece)
+                        piece = jnp.where(lane == at_lane + 65, rest_o, piece)
+                stage, row = message_row(tilt, step)
+                scr[pl.ds(stage * BLOCKS * STAGE_ROWS + row, BLOCKS, stride=STAGE_ROWS), :] = piece
+
+
+def main_kernel(
+    image_ref, left_ref, right_ref, twist_ref, shape_ref, angle_row, angle_ref, dose_ref,
+    lane_tilt, lane_pixel, own_ref, other_ref,
+    cube, scr, x_ref, land, wide, win, acc, part, starts_v, starts_s, cst, trig,
+    a_send, a_recv, x_send, x_recv, m_send, m_recv, sem2, loc, send, recv,
 ):
     v = lax.axis_index("vol")
     t = lax.axis_index("tilt")
@@ -185,16 +204,17 @@
     pl.semaphore_signal(barrier, inc=1, device_id=(v, mate), device_id_type=MESH)
 
     for tilt in range(TILTS_HERE):
-        wide = image_ref[tilt].astype(F32)
+        image = image_ref[tilt].astype(F32)
         for j in range(PIX // 128):
-            cube[pl.ds(tilt * 64 + j, 2, stride=32), :] = wide[:, j * 128 : (j + 1) * 128]
+            cube[pl.ds(tilt * 64 + j, 2, stride=32), :] = image[:, j * 128 : (j + 1) * 128]
 
     operands = (image_ref, left_ref, right_ref, twist_ref, shape_ref, angle_row, angle_ref, dose_ref, cube, scr)
     steps = (0, 1, 7, 2, 6, 3, 5, 4)
-
-    def send_rows(low, high):
-        for block in range(BLOCKS):
-            x_ref[block, low:high] = scr[block * ROWS_MSG + low : block * ROWS_MSG + high, :].astype(BF)
+    size = BLOCKS * STAGE_ROWS
+
+    def send_stage(stage):
+        x_ref[stage] = scr[stage * size : (stage + 1) * size, :].astype(BF).reshape(BLOCKS, STAGE_ROWS, 128)
+        pltpu.make_async_copy(x_ref.at[stage, v], land.at[stage, t, v], a_recv.at[stage, 0, lax.div(z, 4)]).start()
         for dz in steps:
             for far in range(2):
                 for dy in range(4):
@@ -203,157 +223,181 @@
                     zz, yy = lax.rem(z + dz, 8), lax.rem(y + dy, 4)
                     p = (xh if far == 0 else 1 - xh) * 32 + zz * 4 + yy
                     pltpu.make_async_remote_copy(
-                        x_ref.at[p, pl.ds(low, high - low)],
-                        o_ref.at[t, v, pl.ds(low, high - low)],
+                        x_ref.at[stage, p],
+                        land.at[stage, t, v],
                         a_send,
-                        a_recv.at[far, z],
+                        a_recv.at[stage, far, lax.div(z, 4)],
                         device_id=(p, t if far == 0 else cross),
                         device_id_type=MESH,
                     ).start()
 
-    filter_pairs(range(0, 3), *operands)
-    pl.semaphore_wait(barrier, 65)
-    send_rows(0, 16)
-    filter_pairs(range(3, 8), *operands)
-    send_rows(16, 48)
-    own = pltpu.make_async_copy(x_ref.at[v], o_ref.at[t, v], loc_sem)
-    own.start()
-    for dz in steps:
-        for far in range(2):
-            zz = lax.rem(z + 8 - dz, 8)
-            base = (xh if far == 0 else 1 - xh) * 32 + zz * 4
-            slot = t if far == 0 else cross
-            number = 4
-            if dz == 0 and far == 0:
-                own.wait()
-                number = 3
-            pltpu.make_async_copy(
-                o_ref.at[slot, pl.ds(base, number)], o_ref.at[slot, pl.ds(base, number)], a_recv.at[far, zz]
-            ).wait()
-            block = o_ref.at[slot, pl.ds(base, 4)]
-            pltpu.make_async_remote_copy(
-                block, block, x_send, x_recv.at[far, zz], device_id=(v, cross), device_id_type=MESH
-            ).start()
-            pltpu.make_async_remote_copy(
-                block, block, m_send, m_recv.at[0, far, zz], device_id=(v, mate), device_id_type=MESH
-            ).start()
-    for dz in steps:
-        for far in range(2):
-            zz = lax.rem(z + 8 - dz, 8)
-            base = (xh if far == 0 else 1 - xh) * 32 + zz * 4
-            slot = cross if far == 0 else t
-            block = o_ref.at[slot, pl.ds(base, 4)]
-            pltpu.make_async_copy(block, block, x_recv.at[far, zz]).wait()
-            pltpu.make_async_remote_copy(
-                block, block, m_send, m_recv.at[1, far, zz], device_id=(v, mate), device_id_type=MESH
-            ).start()
-    mate_cross = (1 - xl) * 2 + (1 - core)
-    for kind in range(2):
-        for far in range(2):
-            for zz in range(8):
-                base = (xh if far == 0 else 1 - xh) * 32 + zz * 4
-                slot = mate if (kind + far) % 2 == 0 else mate_cross
-                block = o_ref.at[slot, pl.ds(base, 4)]
-                pltpu.make_async_copy(block, block, m_recv.at[kind, far, zz]).wait()
-    pltpu.make_async_copy(x_ref.at[pl.ds(0, 63)], x_ref.at[pl.ds(0, 63)], a_send).wait()
-    half = o_ref.at[0]
-    pltpu.make_async_copy(half, half, x_send).wait()
-    both = o_ref.at[pl.ds(0, 2)]
-    pltpu.make_async_copy(both, both, m_send).wait()
-
-
-def project_kernel(
-    recv_ref, lane_tilt, lane_pixel, own_ref, other_ref,
-    land, scr, win, starts_v, starts_s, cst, trig, part, sem, sem2, loc, send, recv,
-):
-    v = lax.axis_index("vol")
-    t = lax.axis_index("tilt")
-    core = lax.rem(t, 2)
-    mate = (t // 2) * 2 + (1 - core)
-    barrier = pltpu.get_barrier_semaphore()
-    pl.semaphore_signal(barrier, inc=1, device_id=(v, mate), device_id_type=MESH)
-    size = BLOCKS * ROWS_MSG
-    arrive = [pltpu.make_async_copy(recv_ref.at[g], land.at[g], sem.at[g]) for g in range(4)]
-    for copy in arrive:
-        copy.start()
+    def chunk_of(i):
+        far = lax.rem(i, 2)
+        half = lax.rem(lax.div(z, 4) + lax.div(i, 2), 2)
+        base = lax.rem(xh + far, 2) * 32 + half * 16
+        near_slot = lax.rem(xl + far, 2) * 2 + core
+        far_slot = lax.rem(xl + far + 1, 2) * 2 + core
+        return far, half, base, near_slot, far_slot
+
+    def pass_first(stage, i):
+        far, zz, base, slot, _ = chunk_of(i)
+        block = land.at[stage, slot, pl.ds(base, 16)]
+        pltpu.make_async_copy(block, block, a_recv.at[stage, far, zz]).wait()
+        pltpu.make_async_remote_copy(
+            block, block, x_send, x_recv.at[stage, far, zz], device_id=(v, cross), device_id_type=MESH
+        ).start()
+        pltpu.make_async_remote_copy(
+            block, block, m_send, m_recv.at[stage], device_id=(v, mate), device_id_type=MESH
+        ).start()
+
+    def pass_second(stage, i):
+        far, zz, base, _, slot = chunk_of(i)
+        block = land.at[stage, slot, pl.ds(base, 16)]
+        pltpu.make_async_copy(block, block, x_recv.at[stage, far, zz]).wait()
+        pltpu.make_async_remote_copy(
+            block, block, m_send, m_recv.at[stage], device_id=(v, mate), device_id_type=MESH
+        ).start()
+
     lane = lax.broadcasted_iota(jnp.int32, (BLOCKS, 128), 1)
     low = lane < EDGE
     fold = (
         lax.broadcasted_iota(jnp.int32, (EDGE, 128), 0) == (lane & (EDGE - 1))
     ).astype(F32).astype(BF)
-    for group in range(4):
-        arrive[group].wait()
-        scr[group * size : (group + 1) * size, :] = land[group].reshape(size, 128).astype(F32)
-
-    heads = [scr[pl.ds(g * size + 2, TILTS_HERE, stride=3), :] for g in range(4)]
-    heads = jnp.concatenate(heads + [jnp.zeros((128 - TILTS, 128), F32)], axis=0).T
-    tenths = heads[60:61] * 32.0 + heads[61:62]
-    base = heads[62:63] * 64.0 + heads[63:64]
-    cosine, sine = trig_of(tenths)
-    number = lax.broadcasted_iota(jnp.int32, (32, 128), 0)
-    x_tile = ((number >> 3) * TILE + (v + core) * COLS).astype(F32)
-    z_tile = ((number & 7) * TILE).astype(F32)
-    coord = PIX / 2 + (x_tile - PIX / 2) * cosine + (z_tile - DEPTH / 2) * sine
-    local = jnp.floor(coord + jnp.minimum((TILE - 1) * sine, 0.0)) - base
-    local = jnp.clip(local.astype(jnp.int32), 0, BAND - 8 - WIN)
-    tilt_lane = jnp.minimum(lax.broadcasted_iota(jnp.int32, (32, 128), 1), TILTS - 1)
-    starts_v[...] = tilt_lane * BAND + local
-    to_smem = pltpu.make_async_copy(starts_v, starts_s, sem2)
-    to_smem.start()
-    offset = coord - (base + local.astype(F32))
-    both = jnp.concatenate([jnp.broadcast_to(cosine, (8, 128)), jnp.broadcast_to(sine, (8, 128))], axis=0)
-    for g in range(LANES // 128):
-        lanes = slice(g * 128, (g + 1) * 128)
-        which = jnp.broadcast_to(lane_tilt[0:1, lanes], (32, 128))
-        cst[:, lanes] = jnp.take_along_axis(offset, which, axis=1) - lane_pixel[0:1, lanes]
-        trig[:, lanes] = jnp.take_along_axis(both, which[0:16], axis=1)
-
-    batch = 16
-
-    def turn(group, carry):
-        wide = []
-        for b in range(batch):
-            for step in range(3):
-                piece = scr[pl.ds(group * size + b * 3 + step, BLOCKS, stride=ROWS_MSG), :]
-                wide += [jnp.where(low, piece, 0.0).astype(BF), jnp.where(low, 0.0, piece).astype(BF)]
-        turned = dot_t(fold, jnp.concatenate(wide, axis=0))
-        for i in range(3 * batch):
-            at = pl.multiple_of(group * (batch * BAND) + i * EDGE, EDGE)
-            win[pl.ds(at, EDGE), :] = turned[:, i * 128 : (i + 1) * 128]
+
+    def arrive(stage):
+        both = land.at[stage, pl.ds(0, 2)]
+        pltpu.make_async_copy(both, both, m_recv.at[stage]).wait()
+        for group in range(4):
+            wide[group * size : (group + 1) * size, :] = land[stage, group].reshape(size, 128).astype(F32)
+
+    def turn(stage, group, carry):
+        pieces = []
+        for row in range(STAGE_ROWS):
+            piece = wide[pl.ds(group * size + row, BLOCKS, stride=STAGE_ROWS), :]
+            pieces += [jnp.where(low, piece, 0.0).astype(BF), jnp.where(low, 0.0, piece).astype(BF)]
+        turned = dot_t(fold, jnp.concatenate(pieces, axis=0))
+        for row in range(STAGE_ROWS):
+            tilt, step = (SPLIT, stage) if row == 15 else (STAGE_TILTS[stage][row // 3], row % 3)
+            at = pl.multiple_of(group * (TILTS_HERE * BAND) + tilt * BAND + step * EDGE, EDGE)
+            win[pl.ds(at, EDGE), :] = turned[:, row * 128 : (row + 1) * 128]
         return carry
 
-    lax.fori_loop(0, 4, turn, 0)
-    to_smem.wait()
-
-    zcol = lax.broadcasted_iota(jnp.int32, (TILE, 256), 0).astype(F32)
-
-    def tile(number, carry):
-        right = jnp.concatenate(
-            [win[pl.ds(starts_s[number, i], WIN), :] for i in range(TILTS)], axis=0
-        ).astype(BF)
-        total = jnp.zeros((TILE * TILE, 128), F32)
-        for chunk in range(LANES // 256):
-            lanes = slice(chunk * 256, (chunk + 1) * 256)
+    def parameters():
+        heads = [wide[pl.ds(g * size + 2, 4, stride=3), :] for g in range(4)]
+        heads = jnp.concatenate(heads + [jnp.zeros((112, 128), F32)], axis=0).T
+
+        def spread(at):
+            place = lax.broadcasted_iota(jnp.int32, (1, 128), 1)
+            row = heads[at : at + 1]
+            for j in range(1, 4):
+                moved = pltpu.roll(jnp.broadcast_to(heads[at + 2 * j : at + 2 * j + 1], (8, 128)), 16 * j, 1)
+                row = jnp.where((place >= 16 * j) & (place < 16 * j + 16), moved[0:1], row)
+            return row
+
+        tenths = spread(META) * 32.0 + spread(META + 1)
+        base = spread(META + 64) * 64.0 + spread(META + 65)
+        cosine, sine = trig_of(tenths)
+        number = lax.broadcasted_iota(jnp.int32, (32, 128), 0)
+        x_tile = ((number >> 3) * TILE + (v + core) * COLS).astype(F32)
+        z_tile = ((number & 7) * TILE).astype(F32)
+        coord = PIX / 2 + (x_tile - PIX / 2) * cosine + (z_tile - DEPTH / 2) * sine
+        local = jnp.floor(coord + jnp.minimum((TILE - 1) * sine, 0.0)) - base
+        local = jnp.clip(local.astype(jnp.int32), 0, BAND - 8 - WIN)
+        place = lax.broadcasted_iota(jnp.int32, (32, 128), 1) & 63
+        tilt_number = ((place >> 2) & 3) * TILTS_HERE + (place & 3) * 4 + (place >> 4)
+        starts_v[...] = tilt_number * BAND + local
+        to_smem = pltpu.make_async_copy(starts_v, starts_s, sem2)
+        to_smem.start()
+        offset = coord - (base + local.astype(F32))
+        both = jnp.concatenate(
+            [jnp.broadcast_to(cosine, (8, 128)), jnp.broadcast_to(sine, (8, 128))], axis=0
+        )
+        for g in range(STAGE_LANES[3] // 128):
+            lanes = slice(g * 128, (g + 1) * 128)
+            which = jnp.broadcast_to(lane_tilt[0:1, lanes], (32, 128))
+            cst[:, lanes] = jnp.take_along_axis(offset, which, axis=1) - lane_pixel[0:1, lanes]
+            trig[:, lanes] = jnp.take_along_axis(both, which[0:16], axis=1)
+        to_smem.wait()
+
+    def tile(stage, number, carry):
+        chunks = STAGE_CHUNKS[stage]
+        tilts = [(g, a) for g in range(4) for a in STAGE_TILTS[stage]]
+        pad = sum(chunks) - WIN * len(tilts)
+        right = [win[pl.ds(starts_s[number, 16 * (a % 4) + 4 * g + a // 4], WIN), :] for g, a in tilts]
+        right = jnp.concatenate(right + [jnp.zeros((pad, 128), F32)], axis=0).astype(BF)
+        here_rows = pl.ds(pl.multiple_of(number * 256, 256), 256)
+        total = None if stage == 0 else acc[here_rows, :]
+        at = 0
+        origin = cst[pl.ds(number, 1), STAGE_LANES[stage] : STAGE_LANES[stage + 1]]
+        for length in chunks:
+            lanes = slice(STAGE_LANES[stage] + at, STAGE_LANES[stage] + at + length)
             cos_l = trig[0:1, lanes]
-            here = zcol * trig[8:9, lanes] + cst[pl.ds(number, 1), lanes]
+            zcol = lax.broadcasted_iota(jnp.int32, (TILE, length), 0).astype(F32)
+            here = zcol * trig[8:9, lanes] + origin[:, at : at + length]
             pieces = []
             for _ in range(TILE):
-                pieces.append(jnp.maximum(1.0 - jnp.abs(here), 0.0).astype(BF))
+                pieces.append(jnp.maximum(1.0 - jnp.abs(here.astype(BF)), jnp.zeros((), BF)))
                 here = here + cos_l
-            total = total + dot(jnp.concatenate(pieces, axis=0), right[lanes])
+            more = dot(jnp.concatenate(pieces, axis=0), right[at : at + length])
+            total = more if total is None else total + more
+            at += length
+        if stage < 2:
+            acc[here_rows, :] = total
+            return carry
         rounded = total.astype(BF)
         xt, zt = number // 8, lax.rem(number, 8)
         for i in range(TILE):
-            at = pl.multiple_of((xt * TILE + i) * DEPTH + zt * TILE, TILE)
-            part[pl.ds(at, TILE), :] = rounded[i * TILE : (i + 1) * TILE]
+            row = pl.multiple_of((xt * TILE + i) * DEPTH + zt * TILE, TILE)
+            part[pl.ds(row, TILE), :] = rounded[i * TILE : (i + 1) * TILE]
         return carry
+
+    filter_pairs(range(0, 3), *operands)
+    pl.semaphore_wait(barrier, 65)
+    send_stage(0)
+    filter_pairs(range(3, 6), *operands)
+    send_stage(1)
+    filter_pairs(range(6, 8), *operands)
+    send_stage(2)
+
+    def loop_first(stage):
+        def body(i, carry):
+            pass_first(stage, i)
+            return carry
+
+        lax.fori_loop(0, 4, body, 0)
+
+    def loop_second(stage):
+        def body(i, carry):
+            pass_second(stage, i)
+            return carry
+
+        lax.fori_loop(0, 4, body, 0)
+
+    def spread_tiles(stage, low, high):
+        lax.fori_loop(low, high, functools.partial(tile, stage), 0, unroll=2)
+
+    loop_first(0)
+    loop_second(0)
+    loop_first(1)
+    arrive(0)
+    parameters()
+    lax.fori_loop(0, 4, functools.partial(turn, 0), 0)
+    spread_tiles(0, 0, 16)
+    loop_second(1)
+    loop_first(2)
+    spread_tiles(0, 16, 32)
+    arrive(1)
+    lax.fori_loop(0, 4, functools.partial(turn, 1), 0)
+    spread_tiles(1, 0, 16)
+    loop_second(2)
+    spread_tiles(1, 16, 32)
+    arrive(2)
+    lax.fori_loop(0, 4, functools.partial(turn, 2), 0)
 
     span = TILE * DEPTH
     copies = []
     for xt in range(4):
-        lax.fori_loop(8 * xt, 8 * xt + 8, tile, 0)
-        if xt == 0:
-            pl.semaphore_wait(barrier, 1)
+        spread_tiles(2, 8 * xt, 8 * xt + 8)
         slab = pl.ds(xt * span, span)
         there = pltpu.make_async_remote_copy(
             part.at[slab], other_ref.at[slab], send.at[xt], recv.at[xt],
@@ -365,6 +409,12 @@
         copies += [there, here]
     for copy in copies:
         copy.wait()
+    sent = x_ref.at[:, pl.ds(0, 63)]
+    pltpu.make_async_copy(sent, sent, a_send).wait()
+    half = land.at[:, 0]
+    pltpu.make_async_copy(half, half, x_send).wait()
+    both = land.at[:, pl.ds(0, 2)]
+    pltpu.make_async_copy(both, both, m_send).wait()
 
 
 def box_kernel(own_ref, other_ref, corner_ref, owner_ref, box_out, vol_out, land, ext, lines, box_ref, vol_ref, sem, out_sem):
@@ -440,51 +490,41 @@
     anym = pl.BlockSpec(memory_space=pl.ANY)
     dma = pltpu.SemaphoreType.DMA
     tables = [jnp.asarray(a) for a in fft_tables()]
-    recv = pl.pallas_call(
-        exchange_kernel,
-        out_shape=jax.ShapeDtypeStruct((4, BLOCKS, ROWS_MSG, 128), BF),
-        in_specs=[vm] * 6 + [sm] * 2,
-        out_specs=anym,
+    lane_tilt = np.zeros(STAGE_LANES[3], np.int32)
+    lane_pixel = np.full(STAGE_LANES[3], -1.0e4, np.float32)
+    for stage in range(3):
+        tilts = [16 * (a % 4) + 4 * g + a // 4 for g in range(4) for a in STAGE_TILTS[stage]]
+        at, count = STAGE_LANES[stage], WIN * len(tilts)
+        lane_tilt[at : at + count] = np.repeat(np.array(tilts), WIN)
+        lane_pixel[at : at + count] = np.tile(np.arange(WIN), len(tilts))
+    lane_tilt = jnp.asarray(np.stack([lane_tilt] * 8))
+    lane_pixel = jnp.asarray(np.stack([lane_pixel] * 8))
+    part, other = pl.pallas_call(
+        main_kernel,
+        out_shape=(jax.ShapeDtypeStruct((CELLS // 2, 128), BF),) * 2,
+        in_specs=[vm] * 6 + [sm] * 2 + [vm] * 2,
+        out_specs=(anym, anym),
         scratch_shapes=[
             pltpu.VMEM((32 * 32, 128), F32),
-            pltpu.VMEM((BLOCKS * ROWS_MSG, 128), F32),
-            pltpu.VMEM((BLOCKS, ROWS_MSG, 128), BF),
-            dma, dma, dma((2, 8)), dma, dma((2, 8)), dma, dma((2, 2, 8)),
+            pltpu.VMEM((3 * BLOCKS * STAGE_ROWS, 128), F32),
+            pltpu.VMEM((3, BLOCKS, STAGE_ROWS, 128), BF),
+            pltpu.VMEM((3, 4, BLOCKS, STAGE_ROWS, 128), BF),
+            pltpu.VMEM((4 * BLOCKS * STAGE_ROWS, 128), F32),
+            pltpu.VMEM((TILTS * BAND, 128), F32),
+            pltpu.VMEM((CELLS // 2, 128), F32),
+            pltpu.VMEM((CELLS // 2, 128), BF),
+            pltpu.VMEM((32, 128), jnp.int32),
+            pltpu.SMEM((32, 128), jnp.int32),
+            pltpu.VMEM((32, STAGE_LANES[3]), F32),
+            pltpu.VMEM((16, STAGE_LANES[3]), F32),
+            dma, dma((3, 2, 2)), dma, dma((3, 2, 2)), dma, dma((3,)),
+            dma, dma((4,)), dma((4,)), dma((4,)),
         ],
         compiler_params=pltpu.CompilerParams(
             vmem_limit_bytes=VMEM_LIMIT, collective_id=1, has_side_effects=True
         ),
-        name="exchange",
-    )(images, *tables, angle_tenths.reshape(1, TILTS_HERE), angle_tenths, dose_index)
-
-    lanes = np.arange(LANES)
-    lane_tilt = jnp.asarray(np.broadcast_to(lanes // WIN, (8, LANES)).astype(np.int32))
-    lane_pixel = jnp.asarray(np.broadcast_to(lanes % WIN, (8, LANES)).astype(np.float32))
-    part, other = pl.pallas_call(
-        project_kernel,
-        out_shape=(jax.ShapeDtypeStruct((CELLS // 2, 128), BF),) * 2,
-        in_specs=[anym, vm, vm],
-        out_specs=(anym, anym),
-        scratch_shapes=[
-            pltpu.VMEM((4, BLOCKS, ROWS_MSG, 128), BF),
-            pltpu.VMEM((4 * BLOCKS * ROWS_MSG, 128), F32),
-            pltpu.VMEM((TILTS * BAND, 128), F32),
-            pltpu.VMEM((32, 128), jnp.int32),
-            pltpu.SMEM((32, 128), jnp.int32),
-            pltpu.VMEM((32, LANES), F32),
-            pltpu.VMEM((16, LANES), F32),
-            pltpu.VMEM((CELLS // 2, 128), BF),
-            dma((4,)),
-            dma,
-            dma((4,)),
-            dma((4,)),
-            dma((4,)),
-        ],
-        compiler_params=pltpu.CompilerParams(
-            vmem_limit_bytes=VMEM_LIMIT, collective_id=2, has_side_effects=True
-        ),
-        name="project",
-    )(recv, lane_tilt, lane_pixel)
+        name="main",
+    )(images, *tables, angle_tenths.reshape(1, TILTS_HERE), angle_tenths, dose_index, lane_tilt, lane_pixel)
 
     boxes, volume = pl.pallas_call(
         box_kernel,

time: 75.9 us -> 63.8 us (0.84)
  Pallas kernels: 75.1 us -> 63 us
    pallas_call x2 -> x1, Pallas kernels: 65.9 us -> 53.8 us  [per_device(): pl.pallas_call(main_kernel, out_shape=(jax.ShapeDtypeStruct((CELLS // 2,...]
where the time goes in v3:
time: 63.8 us; the launch traced here: 63.6 us
  Pallas kernels  63 us (99%)
  between operations  0.64 us (1%)
    pallas_call x1, Pallas kernels, per_device(): pl.pallas_call(main_kernel, out_shape=(jax.ShapeDtypeStruct((CELLS // 2,...  53.8 us
    pallas_call x1, Pallas kernels, per_device(): pl.pallas_call(box_kernel, out_shape=(jax.ShapeDtypeStruct((4, BOX, BOX *...  9.18 us

profile of v3, /device:TPU:1, one launch (start us, length us, event | category | flops | bytes accessed | tf_op | source)
XLA Modules:
  0.0 63.6 jit_solution(6369000450328926788)
XLA Ops:
  0.6 53.8 %main.1 = (bf16[8192,128]{1,0:T(8,128)(2,1)}, bf16[8192,128]{1,0:T(8,128)(2,1)}) custom-call(bf16[16,2,4096]{2,1,0:T(2,128)(2,1)} %image_ref.1, bf16[2,256,64]{2,1,0:T(8,128)(2,1)} %constant.12.clone.left_ref, bf16[4,256,256]{2,1,0:T(8,128)(2,1)} %constant.13.clone.right_ref, f32[2,64,128]{2,1,0:T(8,128)} %constant.14.clone.twist_ref, ...), custom_call_target="tpu_custom_call" | custom-call | tf_op jit(solution)/shard_map/main/pallas_call | solution.py:502
  54.5 9.2 %boxes.1 = (bf16[4,64,4096]{2,1,0:T(8,128)(2,1)}, bf16[32,64,128]{2,1,0:T(8,128)(2,1)}) custom-call(bf16[8192,128]{1,0:T(8,128)(2,1)} %get-tuple-element.6.own_ref, bf16[8192,128]{1,0:T(8,128)(2,1)} %get-tuple-element.7.other_ref, s32[3,8]{1,0:T(4,128)} %corner_ref.1, s32[1,8]{1,0:T(1,128)} %bitcast.4), custom_call_target="tpu_custom_call" | custom-call | tf_op jit(solution)/shard_map/boxes/pallas_call | solution.py:529

commit v4 on v3

--- a/solution.py
+++ b/solution.py
@@ -214,7 +214,7 @@
 
     def send_stage(stage):
         x_ref[stage] = scr[stage * size : (stage + 1) * size, :].astype(BF).reshape(BLOCKS, STAGE_ROWS, 128)
-        pltpu.make_async_copy(x_ref.at[stage, v], land.at[stage, t, v], a_recv.at[stage, 0, lax.div(z, 4)]).start()
+        pltpu.make_async_copy(x_ref.at[stage, v], land.at[stage, t, v], a_recv.at[stage, 0, lax.div(z, 2)]).start()
         for dz in steps:
             for far in range(2):
                 for dy in range(4):
@@ -226,22 +226,25 @@
                         x_ref.at[stage, p],
                         land.at[stage, t, v],
                         a_send,
-                        a_recv.at[stage, far, lax.div(z, 4)],
+                        a_recv.at[stage, far, lax.div(z, 2)],
                         device_id=(p, t if far == 0 else cross),
                         device_id_type=MESH,
                     ).start()
 
     def chunk_of(i):
         far = lax.rem(i, 2)
-        half = lax.rem(lax.div(z, 4) + lax.div(i, 2), 2)
-        base = lax.rem(xh + far, 2) * 32 + half * 16
+        k = lax.div(i, 2)
+        odd = lax.rem(k, 2)
+        off = odd * lax.div(k + 1, 2) + (1 - odd) * lax.rem(4 - lax.div(k, 2), 4)
+        planes = lax.rem(lax.div(z, 2) + off, 4)
+        base = lax.rem(xh + far, 2) * 32 + planes * 8
         near_slot = lax.rem(xl + far, 2) * 2 + core
         far_slot = lax.rem(xl + far + 1, 2) * 2 + core
-        return far, half, base, near_slot, far_slot
+        return far, planes, base, near_slot, far_slot
 
     def pass_first(stage, i):
         far, zz, base, slot, _ = chunk_of(i)
-        block = land.at[stage, slot, pl.ds(base, 16)]
+        block = land.at[stage, slot, pl.ds(base, 8)]
         pltpu.make_async_copy(block, block, a_recv.at[stage, far, zz]).wait()
         pltpu.make_async_remote_copy(
             block, block, x_send, x_recv.at[stage, far, zz], device_id=(v, cross), device_id_type=MESH
@@ -252,7 +255,7 @@
 
     def pass_second(stage, i):
         far, zz, base, _, slot = chunk_of(i)
-        block = land.at[stage, slot, pl.ds(base, 16)]
+        block = land.at[stage, slot, pl.ds(base, 8)]
         pltpu.make_async_copy(block, block, x_recv.at[stage, far, zz]).wait()
         pltpu.make_async_remote_copy(
             block, block, m_send, m_recv.at[stage], device_id=(v, mate), device_id_type=MESH
@@ -351,6 +354,26 @@
             part[pl.ds(row, TILE), :] = rounded[i * TILE : (i + 1) * TILE]
         return carry
 
+    def first(stage, low, high):
+        def body(i, carry):
+            pass_first(stage, i)
+            return carry
+
+        lax.fori_loop(low, high, body, 0)
+
+    def second(stage):
+        def body(i, carry):
+            pass_second(stage, i)
+            return carry
+
+        lax.fori_loop(0, 8, body, 0)
+
+    def turns(stage):
+        lax.fori_loop(0, 4, functools.partial(turn, stage), 0, unroll=2)
+
+    def tiles(stage, low, high):
+        lax.fori_loop(low, high, functools.partial(tile, stage), 0, unroll=4)
+
     filter_pairs(range(0, 3), *operands)
     pl.semaphore_wait(barrier, 65)
     send_stage(0)
@@ -358,46 +381,28 @@
     send_stage(1)
     filter_pairs(range(6, 8), *operands)
     send_stage(2)
-
-    def loop_first(stage):
-        def body(i, carry):
-            pass_first(stage, i)
-            return carry
-
-        lax.fori_loop(0, 4, body, 0)
-
-    def loop_second(stage):
-        def body(i, carry):
-            pass_second(stage, i)
-            return carry
-
-        lax.fori_loop(0, 4, body, 0)
-
-    def spread_tiles(stage, low, high):
-        lax.fori_loop(low, high, functools.partial(tile, stage), 0, unroll=2)
-
-    loop_first(0)
-    loop_second(0)
-    loop_first(1)
+    first(0, 0, 8)
+    second(0)
+    first(1, 0, 8)
     arrive(0)
     parameters()
-    lax.fori_loop(0, 4, functools.partial(turn, 0), 0)
-    spread_tiles(0, 0, 16)
-    loop_second(1)
-    loop_first(2)
-    spread_tiles(0, 16, 32)
+    turns(0)
+    tiles(0, 0, 16)
+    second(1)
+    first(2, 0, 8)
+    tiles(0, 16, 32)
     arrive(1)
-    lax.fori_loop(0, 4, functools.partial(turn, 1), 0)
-    spread_tiles(1, 0, 16)
-    loop_second(2)
-    spread_tiles(1, 16, 32)
+    turns(1)
+    tiles(1, 0, 16)
+    second(2)
+    tiles(1, 16, 32)
     arrive(2)
-    lax.fori_loop(0, 4, functools.partial(turn, 2), 0)
+    turns(2)
 
     span = TILE * DEPTH
     copies = []
     for xt in range(4):
-        spread_tiles(2, 8 * xt, 8 * xt + 8)
+        tiles(2, 8 * xt, 8 * xt + 8)
         slab = pl.ds(xt * span, span)
         there = pltpu.make_async_remote_copy(
             part.at[slab], other_ref.at[slab], send.at[xt], recv.at[xt],
@@ -472,7 +477,7 @@
             box_ref[slot, :, pl.ds(pl.multiple_of(i * 512, 512), 512)] = dot_t(chosen, rows).astype(BF)
             return carry
 
-        lax.fori_loop(0, BOX // 8, cut, 0, unroll=2)
+        lax.fori_loop(0, BOX // 8, cut, 0, unroll=8)
         copies.append(pltpu.make_async_copy(box_ref.at[slot], box_out.at[slot], out_sem.at[slot]))
         copies[-1].start()
     for copy in copies:
@@ -517,7 +522,7 @@
             pltpu.SMEM((32, 128), jnp.int32),
             pltpu.VMEM((32, STAGE_LANES[3]), F32),
             pltpu.VMEM((16, STAGE_LANES[3]), F32),
-            dma, dma((3, 2, 2)), dma, dma((3, 2, 2)), dma, dma((3,)),
+            dma, dma((3, 2, 4)), dma, dma((3, 2, 4)), dma, dma((3,)),
             dma, dma((4,)), dma((4,)), dma((4,)),
         ],
         compiler_params=pltpu.CompilerParams(

time: 63.8 us -> 59.4 us (0.931)
  Pallas kernels: 63 us -> 58.6 us
    pallas_call x1, Pallas kernels: 53.8 us -> 51.3 us  [per_device(): pl.pallas_call(main_kernel, out_shape=(jax.ShapeDtypeStruct((CELLS // 2,...]
    pallas_call x1, Pallas kernels: 9.18 us -> 7.27 us  [per_device(): pl.pallas_call(box_kernel, out_shape=(jax.ShapeDtypeStruct((4, BOX, BOX *...]
where the time goes in v4:
time: 59.4 us; the launch traced here: 59.2 us
  Pallas kernels  58.6 us (99%)
  between operations  0.64 us (1%)
    pallas_call x1, Pallas kernels, per_device(): pl.pallas_call(main_kernel, out_shape=(jax.ShapeDtypeStruct((CELLS // 2,...  51.3 us
    pallas_call x1, Pallas kernels, per_device(): pl.pallas_call(box_kernel, out_shape=(jax.ShapeDtypeStruct((4, BOX, BOX *...  7.27 us

profile of v4, /device:TPU:1, one launch (start us, length us, event | category | flops | bytes accessed | tf_op | source)
XLA Modules:
  0.0 59.2 jit_solution(17412212361653791686)
XLA Ops:
  0.6 51.3 %main.1 = (bf16[8192,128]{1,0:T(8,128)(2,1)}, bf16[8192,128]{1,0:T(8,128)(2,1)}) custom-call(bf16[16,2,4096]{2,1,0:T(2,128)(2,1)} %image_ref.1, bf16[2,256,64]{2,1,0:T(8,128)(2,1)} %constant.12.clone.left_ref, bf16[4,256,256]{2,1,0:T(8,128)(2,1)} %constant.13.clone.right_ref, f32[2,64,128]{2,1,0:T(8,128)} %constant.14.clone.twist_ref, ...), custom_call_target="tpu_custom_call" | custom-call | tf_op jit(solution)/shard_map/main/pallas_call | solution.py:507
  52.0 7.3 %boxes.1 = (bf16[4,64,4096]{2,1,0:T(8,128)(2,1)}, bf16[32,64,128]{2,1,0:T(8,128)(2,1)}) custom-call(bf16[8192,128]{1,0:T(8,128)(2,1)} %get-tuple-element.6.own_ref, bf16[8192,128]{1,0:T(8,128)(2,1)} %get-tuple-element.7.other_ref, s32[3,8]{1,0:T(4,128)} %corner_ref.1, s32[1,8]{1,0:T(1,128)} %bitcast.4), custom_call_target="tpu_custom_call" | custom-call | tf_op jit(solution)/shard_map/boxes/pallas_call | solution.py:534

commit v5 on v4

--- a/solution.py
+++ b/solution.py
@@ -350,8 +350,7 @@
         rounded = total.astype(BF)
         xt, zt = number // 8, lax.rem(number, 8)
         for i in range(TILE):
-            row = pl.multiple_of((xt * TILE + i) * DEPTH + zt * TILE, TILE)
-            part[pl.ds(row, TILE), :] = rounded[i * TILE : (i + 1) * TILE]
+            part[xt * TILE + i, pl.ds(pl.multiple_of(zt * TILE, TILE), TILE), :] = rounded[i * TILE : (i + 1) * TILE]
         return carry
 
     def first(stage, low, high):
@@ -369,7 +368,7 @@
         lax.fori_loop(0, 8, body, 0)
 
     def turns(stage):
-        lax.fori_loop(0, 4, functools.partial(turn, stage), 0, unroll=2)
+        lax.fori_loop(0, 4, functools.partial(turn, stage), 0, unroll=4)
 
     def tiles(stage, low, high):
         lax.fori_loop(low, high, functools.partial(tile, stage), 0, unroll=4)
@@ -389,26 +388,26 @@
     turns(0)
     tiles(0, 0, 16)
     second(1)
-    first(2, 0, 8)
+    first(2, 0, 4)
     tiles(0, 16, 32)
+    first(2, 4, 8)
     arrive(1)
     turns(1)
-    tiles(1, 0, 16)
+    tiles(1, 0, 24)
     second(2)
-    tiles(1, 16, 32)
+    tiles(1, 24, 32)
     arrive(2)
     turns(2)
 
-    span = TILE * DEPTH
     copies = []
-    for xt in range(4):
-        tiles(2, 8 * xt, 8 * xt + 8)
-        slab = pl.ds(xt * span, span)
+    for k in range(8):
+        tiles(2, 4 * k, 4 * k + 4)
+        columns, depths = pl.ds((k // 2) * TILE, TILE), pl.ds((k % 2) * 64, 64)
         there = pltpu.make_async_remote_copy(
-            part.at[slab], other_ref.at[slab], send.at[xt], recv.at[xt],
+            part.at[columns, depths], other_ref.at[columns, depths], send.at[k], recv.at[k],
             device_id=(v, mate), device_id_type=MESH,
         )
-        here = pltpu.make_async_copy(part.at[slab], own_ref.at[slab], loc.at[xt])
+        here = pltpu.make_async_copy(part.at[columns, depths], own_ref.at[columns, depths], loc.at[k])
         there.start()
         here.start()
         copies += [there, here]
@@ -428,8 +427,8 @@
     core = lax.rem(t, 2)
     half = CELLS // 2
     arrive = [
-        pltpu.make_async_copy(own_ref, land.at[core], sem.at[0]),
-        pltpu.make_async_copy(other_ref, land.at[1 - core], sem.at[1]),
+        pltpu.make_async_copy(own_ref, land.at[core], sem.at[core]),
+        pltpu.make_async_copy(other_ref, land.at[1 - core], sem.at[1 - core]),
     ]
     for copy in arrive:
         copy.start()
@@ -440,8 +439,7 @@
     y_of = (lane & 63) * 2 + (lane >> 6)
     line = lax.broadcasted_iota(jnp.int32, (BOX, 128), 0)
     quarter = (y_of == line + t * 32).astype(F32).astype(BF)[0:32]
-    for copy in arrive:
-        copy.wait()
+    pltpu.make_async_copy(own_ref, land.at[0], sem.at[0]).wait()
 
     def slab(i, carry):
         rows = land[0, pl.ds(pl.multiple_of(i * 1024, 1024), 1024), :]
@@ -450,12 +448,14 @@
             lines[pl.ds(i * 8 + j, 32, stride=COLS), :] = both[:, j * 128 : (j + 1) * 128]
         return carry
 
-    lax.fori_loop(0, COLS // 8, slab, 0, unroll=2)
+    lax.fori_loop(0, COLS // 8, slab, 0, unroll=8)
     for i in range(32):
         vol_ref[i] = lines[i * COLS : (i + 1) * COLS, :].astype(BF)
     copies = [pltpu.make_async_copy(vol_ref, vol_out, out_sem.at[4])]
     copies[0].start()
     for side in range(2):
+        if side == 1:
+            pltpu.make_async_copy(own_ref, land.at[1], sem.at[1]).wait()
         for i in range(8):
             ext[side * half + i * 1024 : side * half + (i + 1) * 1024, :] = land[
                 side, i * 1024 : (i + 1) * 1024
@@ -506,7 +506,7 @@
     lane_pixel = jnp.asarray(np.stack([lane_pixel] * 8))
     part, other = pl.pallas_call(
         main_kernel,
-        out_shape=(jax.ShapeDtypeStruct((CELLS // 2, 128), BF),) * 2,
+        out_shape=(jax.ShapeDtypeStruct((COLS, DEPTH, 128), BF),) * 2,
         in_specs=[vm] * 6 + [sm] * 2 + [vm] * 2,
         out_specs=(anym, anym),
         scratch_shapes=[
@@ -517,13 +517,13 @@
             pltpu.VMEM((4 * BLOCKS * STAGE_ROWS, 128), F32),
             pltpu.VMEM((TILTS * BAND, 128), F32),
             pltpu.VMEM((CELLS // 2, 128), F32),
-            pltpu.VMEM((CELLS // 2, 128), BF),
+            pltpu.VMEM((COLS, DEPTH, 128), BF),
             pltpu.VMEM((32, 128), jnp.int32),
             pltpu.SMEM((32, 128), jnp.int32),
             pltpu.VMEM((32, STAGE_LANES[3]), F32),
             pltpu.VMEM((16, STAGE_LANES[3]), F32),
             dma, dma((3, 2, 4)), dma, dma((3, 2, 4)), dma, dma((3,)),
-            dma, dma((4,)), dma((4,)), dma((4,)),
+            dma, dma((8,)), dma((8,)), dma((8,)),
         ],
         compiler_params=pltpu.CompilerParams(
             vmem_limit_bytes=VMEM_LIMIT, collective_id=1, has_side_effects=True
@@ -550,7 +550,7 @@
         ],
         compiler_params=pltpu.CompilerParams(vmem_limit_bytes=VMEM_LIMIT),
         name="boxes",
-    )(part, other, box_corner, box_owner.T)
+    )(part.reshape(CELLS // 2, 128), other.reshape(CELLS // 2, 128), box_corner, box_owner.T)
     return volume, boxes.reshape(1, 1, 4, BOX, BOX * BOX)
 
 

time: 59.4 us -> 58 us (0.976)
  Pallas kernels: 58.6 us -> 57.1 us
    pallas_call x1, Pallas kernels: 51.3 us -> 50.2 us  [per_device(): pl.pallas_call(main_kernel, out_shape=(jax.ShapeDtypeStruct((COLS, DEPTH,...]
where the time goes in v5:
time: 58 us; the launch traced here: 57.9 us
  Pallas kernels  57.1 us (98%)
  between operations  0.8 us (1%)
    pallas_call x1, Pallas kernels, per_device(): pl.pallas_call(main_kernel, out_shape=(jax.ShapeDtypeStruct((COLS, DEPTH,...  50.2 us
    pallas_call x1, Pallas kernels, per_device(): pl.pallas_call(box_kernel, out_shape=(jax.ShapeDtypeStruct((4, BOX, BOX *...  6.91 us

profile of v5, /device:TPU:1, one launch (start us, length us, event | category | flops | bytes accessed | tf_op | source)
XLA Modules:
  0.0 57.9 jit_solution(5333398269483376477)
XLA Ops:
  0.6 50.2 %main.1 = (bf16[64,128,128]{2,1,0:T(8,128)(2,1)}, bf16[64,128,128]{2,1,0:T(8,128)(2,1)}) custom-call(bf16[16,2,4096]{2,1,0:T(2,128)(2,1)} %image_ref.1, bf16[2,256,64]{2,1,0:T(8,128)(2,1)} %constant.12.clone.left_ref, bf16[4,256,256]{2,1,0:T(8,128)(2,1)} %constant.13.clone.right_ref, f32[2,64,128]{2,1,0:T(8,128)} %constant.14.clone.twist_ref, ...), custom_call_target="tpu_custom_call" | custom-call | tf_op jit(solution)/shard_map/main/pallas_call | solution.py:507
  50.8 6.9 %boxes.1 = (bf16[4,64,4096]{2,1,0:T(8,128)(2,1)}, bf16[32,64,128]{2,1,0:T(8,128)(2,1)}) custom-call(bf16[8192,128]{1,0:T(8,128)(2,1)} %bitcast.5, bf16[8192,128]{1,0:T(8,128)(2,1)} %bitcast.6, s32[3,8]{1,0:T(4,128)} %corner_ref.1, s32[1,8]{1,0:T(1,128)} %bitcast.8), custom_call_target="tpu_custom_call" | custom-call | tf_op jit(solution)/shard_map/boxes/pallas_call | solution.py:534

commit v6 on v5

--- a/solution.py
+++ b/solution.py
@@ -382,9 +382,10 @@
     send_stage(2)
     first(0, 0, 8)
     second(0)
-    first(1, 0, 8)
+    first(1, 0, 4)
     arrive(0)
     parameters()
+    first(1, 4, 8)
     turns(0)
     tiles(0, 0, 16)
     second(1)

time: 58 us -> 58.7 us (1.012)
  Pallas kernels: 57.1 us -> 57.7 us
    pallas_call x1, Pallas kernels: 50.2 us -> 50.8 us  [per_device(): pl.pallas_call(main_kernel, out_shape=(jax.ShapeDtypeStruct((COLS, DEPTH,...]
where the time goes in v6:
time: 58.7 us; the launch traced here: 58.5 us
  Pallas kernels  57.7 us (98%)
  between operations  0.8 us (1%)
    pallas_call x1, Pallas kernels, per_device(): pl.pallas_call(main_kernel, out_shape=(jax.ShapeDtypeStruct((COLS, DEPTH,...  50.8 us
    pallas_call x1, Pallas kernels, per_device(): pl.pallas_call(box_kernel, out_shape=(jax.ShapeDtypeStruct((4, BOX, BOX *...  6.9 us

profile of v6, /device:TPU:1, one launch (start us, length us, event | category | flops | bytes accessed | tf_op | source)
XLA Modules:
  0.0 58.5 jit_solution(3117789879310901017)
XLA Ops:
  0.6 50.8 %main.1 = (bf16[64,128,128]{2,1,0:T(8,128)(2,1)}, bf16[64,128,128]{2,1,0:T(8,128)(2,1)}) custom-call(bf16[16,2,4096]{2,1,0:T(2,128)(2,1)} %image_ref.1, bf16[2,256,64]{2,1,0:T(8,128)(2,1)} %constant.12.clone.left_ref, bf16[4,256,256]{2,1,0:T(8,128)(2,1)} %constant.13.clone.right_ref, f32[2,64,128]{2,1,0:T(8,128)} %constant.14.clone.twist_ref, ...), custom_call_target="tpu_custom_call" | custom-call | tf_op jit(solution)/shard_map/main/pallas_call | solution.py:508
  51.4 6.9 %boxes.1 = (bf16[4,64,4096]{2,1,0:T(8,128)(2,1)}, bf16[32,64,128]{2,1,0:T(8,128)(2,1)}) custom-call(bf16[8192,128]{1,0:T(8,128)(2,1)} %bitcast.5, bf16[8192,128]{1,0:T(8,128)(2,1)} %bitcast.6, s32[3,8]{1,0:T(4,128)} %corner_ref.1, s32[1,8]{1,0:T(1,128)} %bitcast.8), custom_call_target="tpu_custom_call" | custom-call | tf_op jit(solution)/shard_map/boxes/pallas_call | solution.py:535
